TPU v7x, 128 devices: a whole 4x4x4 slice. The times are simulated.
128 devices in a mesh: fsdp: 64 (over y, x_hi, z, core), sp: 2 (over x_lo).
Axes of the slice: x: 4 (x_hi: 2, x_lo: 2; x = x_hi * 2 + x_lo), y: 4, z: 4, core: 2. Of those that a mesh axis runs over, the one named last changes fastest.
Arguments:
- inputs: bfloat16 [16384, 768], P(('fsdp', 'sp')), may hold values from -6 to 6
- cotangent: bfloat16 [16384, 768], P(('fsdp', 'sp')), may hold values from -6 to 6
- routes: int32 [16384, 1], P(('fsdp', 'sp')), may hold values from 0 to 15; in each aligned block of 128 rows (0 to 127, 128 to 255, ...) at most 10 rows name the same one
- drop_mask: int32 [16384], P(('fsdp', 'sp')), may hold values 0 or 1
- buckets: int32 [511], replicated, may hold values from 0 to 31
- qkv_weight: bfloat16 [768, 2304], P(('fsdp', 'sp')), may hold values from -0.078125 to 0.078125
- out_weight: bfloat16 [768, 768], P(('fsdp', 'sp')), may hold values from -3.5 to 3.5
- router_weight: bfloat16 [768, 16], P(('fsdp', 'sp')), may hold values from -0.15625 to 0.15625
- attn_gain: bfloat16 [768], P(('fsdp', 'sp')), may hold values from 0.5 to 1.5
- ffn_gain: bfloat16 [768], P(('fsdp', 'sp')), may hold values from 0.5 to 1.5
- bias_table: bfloat16 [384], P(('fsdp', 'sp')), may hold values from -4 to 4
- expert_in: bfloat16 [768, 49152], P(None, ('fsdp', 'sp')), may hold values from -0.21875 to 0.21875
- expert_out: bfloat16 [49152, 768], P(('fsdp', 'sp')), may hold values from -1.75 to 1.75
Outputs:
- result: bfloat16 [16384, 768], P(('fsdp', 'sp'))
- grad_input: bfloat16 [16384, 768], P(('fsdp', 'sp'))
- grad_qkv: float32 [768, 2304], P(('fsdp', 'sp'))
- grad_out_weight: float32 [768, 768], P(('fsdp', 'sp'))
- grad_router: float32 [768, 16], P(('fsdp', 'sp'))
- grad_attn_gain: float32 [768], P(('fsdp', 'sp'))
- grad_ffn_gain: float32 [768], P(('fsdp', 'sp'))
- grad_bias: float32 [384], P(('fsdp', 'sp'))
- grad_expert_in: float32 [768, 49152], P(None, ('fsdp', 'sp'))
- grad_expert_out: float32 [49152, 768], P(('fsdp', 'sp'))
Inputs may be any that keep to these rules, and one draw needn't show every extreme that they name: `routes`: among the 128 tokens of one device no expert is named more than 10 times, a bound that some block reaches.
All inputs are finite; a program needn't handle non-finite values. No bound on the sum of `drop_mask` on one device may be relied on, other than what follows from the above.
Results may differ from a plain program's by a relative error of at most 0.03.
Values may be sent and summed in bfloat16 or wider, within the bound.
A program may use at most 128 MiB of HBM per device.

v0:
```python
import jax
import jax.numpy as jnp
from jax import lax
from jax.sharding import PartitionSpec as P

HEADS = 12
HEAD_DIM = 64
EXPERTS = 16
BUCKETS = 32
CAP = 10


EPSILON = 1e-06


def rms_norm(values, gain):
    scale = lax.rsqrt(jnp.mean(values * values, axis=-1, keepdims=True) + EPSILON)
    return values * scale * gain


def offset_index(begin_row, row_count, length):
    query_pos = begin_row + jnp.arange(row_count, dtype=jnp.int32)
    key_pos = jnp.arange(length, dtype=jnp.int32)
    return key_pos[None, :] - query_pos[:, None] + length - 1


def body(
    inputs,
    cotangent,
    routes,
    drop_mask,
    buckets,
    qkv_weight,
    out_weight,
    router_weight,
    attn_gain,
    ffn_gain,
    bias_table,
    expert_in,
    expert_out,
):
    tok_rows, width = inputs.shape
    seq_parts = lax.axis_size("sp")
    devices = lax.axis_size(("fsdp", "sp"))
    length = tok_rows * seq_parts
    head_count = HEADS // seq_parts
    head_width = head_count * HEAD_DIM
    copies = devices // EXPERTS
    block_rows = min(512, length)
    block_count = length // block_rows
    block_starts = jnp.arange(block_count, dtype=jnp.int32) * block_rows
    gathered = (
        lax.all_gather(qkv_weight, ("fsdp", "sp"), axis=0, tiled=True),
        lax.all_gather(out_weight, ("fsdp", "sp"), axis=0, tiled=True),
        lax.all_gather(router_weight, ("fsdp", "sp"), axis=0, tiled=True),
        lax.all_gather(attn_gain, ("fsdp", "sp"), axis=0, tiled=True),
        lax.all_gather(ffn_gain, ("fsdp", "sp"), axis=0, tiled=True),
        lax.all_gather(bias_table, ("fsdp", "sp"), axis=0, tiled=True),
    )
    qkv_full, out_full, router_full, gain_one, gain_two, table_full = gathered
    features = inputs.astype(jnp.float32)
    gain_one32 = gain_one.astype(jnp.float32)
    normed = rms_norm(features, gain_one32).astype(jnp.bfloat16)
    projected = jnp.dot(normed, qkv_full, preferred_element_type=jnp.float32).astype(jnp.bfloat16)
    per_head = lax.all_to_all(
        projected.reshape(tok_rows, 3, seq_parts, head_width),
        "sp",
        split_axis=2,
        concat_axis=0,
        tiled=True,
    )
    per_head = per_head.reshape(length, 3, head_count, HEAD_DIM)
    queries = per_head[:, 0]
    keys_all = per_head[:, 1]
    values_all = per_head[:, 2]
    head_start = lax.axis_index("sp") * head_count
    table_mine = lax.dynamic_slice_in_dim(
        table_full.reshape(BUCKETS, HEADS), head_start, head_count, 1
    )
    bucket_ids = jnp.arange(BUCKETS, dtype=jnp.int32)

    def bucket_block(begin_row):
        relative = offset_index(begin_row, block_rows, length).reshape(-1)
        picked = jnp.take(buckets, relative, axis=0).reshape(block_rows, length)
        return (picked[:, :, None] == bucket_ids[None, None, :]).astype(jnp.bfloat16)

    def scores_for(begin_row):
        raw_scores = jnp.einsum(
            "qhd,khd->hqk", queries, keys_all, preferred_element_type=jnp.float32
        )
        bucket_hot = bucket_block(begin_row)
        bias_rows = jnp.einsum(
            "qkb,bh->hqk", bucket_hot, table_mine, preferred_element_type=jnp.float32
        )
        return (raw_scores + bias_rows, queries, bucket_hot)

    def attend(begin_row):
        scores, rows_query, bucket_hot = scores_for(begin_row)
        row_top = jnp.max(scores, axis=-1, keepdims=True)
        exponent = jnp.exp(scores - row_top)
        totals = jnp.sum(exponent, axis=-1, keepdims=True)
        weights = (exponent / totals).astype(jnp.bfloat16)
        mixed_rows = jnp.einsum(
            "hqk,khd->qhd", weights, values_all, preferred_element_type=jnp.float32
        )
        return (mixed_rows.astype(jnp.bfloat16), (row_top + jnp.log(totals))[..., 0])

    mixed_blocks, log_totals = lax.map(attend, block_starts)
    mixed_heads = mixed_blocks.reshape(length, 1, head_width)
    mixed_tok = lax.all_to_all(mixed_heads, "sp", split_axis=0, concat_axis=1, tiled=True).reshape(
        tok_rows, width
    )
    after_attn = features + jnp.dot(mixed_tok, out_full, preferred_element_type=jnp.float32)
    gain_two32 = gain_two.astype(jnp.float32)
    normed_two = rms_norm(after_attn, gain_two32).astype(jnp.bfloat16)
    logits = jnp.dot(normed_two, router_full, preferred_element_type=jnp.float32)
    router_probs = jax.nn.softmax(logits, axis=-1)
    chosen = routes[:, 0]
    expert_hot = chosen[:, None] == jnp.arange(EXPERTS, dtype=jnp.int32)[None, :]
    gates = jnp.sum(jnp.where(expert_hot, router_probs, 0.0), axis=-1)
    kept = drop_mask.astype(jnp.float32)
    running = jnp.cumsum(expert_hot.astype(jnp.int32), axis=0)
    slot_index = jnp.sum(jnp.where(expert_hot, running, 0), axis=-1) - 1
    flat_slot = chosen * CAP + slot_index
    placing = (
        (jnp.arange(EXPERTS * CAP, dtype=jnp.int32)[:, None] == flat_slot[None, :])
        & (drop_mask[None, :] > 0)
    ).astype(jnp.bfloat16)
    outgoing = jnp.dot(placing, normed_two, preferred_element_type=jnp.float32).astype(jnp.bfloat16)
    outgoing = jnp.broadcast_to(
        outgoing.reshape(EXPERTS, 1, CAP, width), (EXPERTS, copies, CAP, width)
    ).reshape(devices, CAP, width)
    arrived_rows = lax.all_to_all(outgoing, ("fsdp", "sp"), split_axis=0, concat_axis=0, tiled=True)
    flat_rows = arrived_rows.reshape(-1, width)
    pre_rows = jnp.dot(flat_rows, expert_in, preferred_element_type=jnp.float32)
    activity = jax.nn.gelu(pre_rows).astype(jnp.bfloat16)
    part_rows = jnp.dot(activity, expert_out, preferred_element_type=jnp.float32).astype(
        jnp.bfloat16
    )
    coming_back = lax.all_to_all(
        part_rows.reshape(arrived_rows.shape),
        ("fsdp", "sp"),
        split_axis=0,
        concat_axis=0,
        tiled=True,
    )
    hidden_pre = pre_rows.reshape(arrived_rows.shape[0], arrived_rows.shape[1], -1)
    slot_out = jnp.sum(
        coming_back.astype(jnp.float32).reshape(EXPERTS, copies, CAP, width), axis=1
    ).reshape(EXPERTS * CAP, width)
    expert_tok = jnp.take(slot_out, flat_slot, axis=0)
    scaled_gate = kept * gates
    result = after_attn + scaled_gate[:, None] * expert_tok
    regathered = (
        lax.all_gather(qkv_weight, ("fsdp", "sp"), axis=0, tiled=True),
        lax.all_gather(out_weight, ("fsdp", "sp"), axis=0, tiled=True),
        lax.all_gather(router_weight, ("fsdp", "sp"), axis=0, tiled=True),
    )
    qkv_full, out_full, router_full = regathered
    grad_result = cotangent.astype(jnp.float32)
    grad_expert_tok = (grad_result * scaled_gate[:, None]).astype(jnp.bfloat16)
    grad_gate = kept * jnp.sum(grad_result * expert_tok, axis=-1)
    grad_logits = (
        (grad_gate * gates)[:, None] * (expert_hot.astype(jnp.float32) - router_probs)
    ).astype(jnp.bfloat16)
    grad_router = jnp.einsum(
        "td,te->de", normed_two, grad_logits, preferred_element_type=jnp.float32
    )
    grad_normed_two = jnp.einsum(
        "te,de->td", grad_logits, router_full, preferred_element_type=jnp.float32
    )
    grad_slots = jnp.dot(placing, grad_expert_tok, preferred_element_type=jnp.float32).astype(
        jnp.bfloat16
    )
    grad_slots = jnp.broadcast_to(
        grad_slots.reshape(EXPERTS, 1, CAP, width), (EXPERTS, copies, CAP, width)
    ).reshape(devices, CAP, width)
    grad_arrived = lax.all_to_all(
        grad_slots, ("fsdp", "sp"), split_axis=0, concat_axis=0, tiled=True
    ).reshape(-1, width)
    rows_in = arrived_rows.reshape(-1, width)
    pre_flat = hidden_pre.reshape(rows_in.shape[0], -1)
    act_value, act_pull = jax.vjp(jax.nn.gelu, pre_flat)
    act_low = act_value.astype(jnp.bfloat16)
    grad_expert_out = jnp.einsum(
        "rf,rd->fd", act_low, grad_arrived, preferred_element_type=jnp.float32
    )
    grad_act = jnp.einsum("rd,fd->rf", grad_arrived, expert_out, preferred_element_type=jnp.float32)
    grad_pre = act_pull(grad_act)[0].astype(jnp.bfloat16)
    grad_expert_in = jnp.einsum("rd,rf->df", rows_in, grad_pre, preferred_element_type=jnp.float32)
    grad_rows = jnp.einsum(
        "rf,df->rd", grad_pre, expert_in, preferred_element_type=jnp.float32
    ).astype(jnp.bfloat16)
    grad_back = lax.all_to_all(
        grad_rows.reshape(devices, CAP, width),
        ("fsdp", "sp"),
        split_axis=0,
        concat_axis=0,
        tiled=True,
    )
    grad_slot_sum = jnp.sum(
        grad_back.astype(jnp.float32).reshape(EXPERTS, copies, CAP, width), axis=1
    ).reshape(EXPERTS * CAP, width)
    grad_normed_two = grad_normed_two + jnp.take(grad_slot_sum, flat_slot, axis=0)
    unused_two, second_pull = jax.vjp(rms_norm, after_attn, gain_two32)
    grad_norm_in, grad_gain_two = second_pull(grad_normed_two)
    grad_after = grad_result + grad_norm_in
    grad_proj = grad_after.astype(jnp.bfloat16)
    grad_out_weight = jnp.einsum(
        "td,te->de", mixed_tok, grad_proj, preferred_element_type=jnp.float32
    )
    grad_mixed = jnp.einsum(
        "te,de->td", grad_proj, out_full, preferred_element_type=jnp.float32
    ).astype(jnp.bfloat16)
    grad_heads = lax.all_to_all(
        grad_mixed.reshape(tok_rows, seq_parts, head_width),
        "sp",
        split_axis=1,
        concat_axis=0,
        tiled=True,
    )
    grad_heads = grad_heads.reshape(length, head_count, HEAD_DIM)

    def attend_back(carry, item):
        grad_keys, grad_values, grad_table_mine = carry
        begin_row, log_rows = item
        scores, rows_query, bucket_hot = scores_for(begin_row)
        probs = jnp.exp(scores - log_rows[..., None])
        probs_low = probs.astype(jnp.bfloat16)
        grad_probs = jnp.einsum(
            "qhd,khd->hqk", grad_heads, values_all, preferred_element_type=jnp.float32
        )
        grad_scores = (
            probs * (grad_probs - jnp.sum(probs * grad_probs, axis=-1, keepdims=True))
        ).astype(jnp.bfloat16)
        grad_query = jnp.einsum(
            "hqk,khd->qhd", grad_scores, keys_all, preferred_element_type=jnp.float32
        )
        grad_keys = grad_keys + jnp.einsum(
            "hqk,qhd->khd", grad_scores, rows_query, preferred_element_type=jnp.float32
        )
        grad_values = grad_values + jnp.einsum(
            "hqk,qhd->khd", probs_low, grad_heads, preferred_element_type=jnp.float32
        )
        grad_table_mine = grad_table_mine + jnp.einsum(
            "hqk,qkb->bh", grad_scores, bucket_hot, preferred_element_type=jnp.float32
        )
        return ((grad_keys, grad_values, grad_table_mine), grad_query.astype(jnp.bfloat16))

    zero_keys = jnp.zeros((length, head_count, HEAD_DIM), jnp.float32)
    start_carry = (zero_keys, zero_keys, jnp.zeros((BUCKETS, head_count), jnp.float32))
    final_carry, grad_queries = lax.scan(attend_back, start_carry, (block_starts, log_totals))
    grad_keys, grad_values, grad_table_mine = final_carry
    grad_stack = jnp.stack(
        [
            grad_queries.reshape(length, head_width),
            grad_keys.reshape(length, head_width).astype(jnp.bfloat16),
            grad_values.reshape(length, head_width).astype(jnp.bfloat16),
        ],
        axis=1,
    )
    grad_projected = lax.all_to_all(
        grad_stack.reshape(length, 3, 1, head_width), "sp", split_axis=0, concat_axis=2, tiled=True
    ).reshape(tok_rows, 3 * width)
    grad_table = lax.dynamic_update_slice_in_dim(
        jnp.zeros((BUCKETS, HEADS), jnp.float32), grad_table_mine, head_start, 1
    ).reshape(-1)
    grad_qkv = jnp.einsum("td,te->de", normed, grad_projected, preferred_element_type=jnp.float32)
    grad_normed = jnp.einsum(
        "te,de->td", grad_projected, qkv_full, preferred_element_type=jnp.float32
    )
    unused_one, first_pull = jax.vjp(rms_norm, features, gain_one32)
    grad_features, grad_gain_one = first_pull(grad_normed)
    grad_input = (grad_after + grad_features).astype(jnp.bfloat16)
    reduced = (
        lax.psum_scatter(grad_qkv, ("fsdp", "sp"), scatter_dimension=0, tiled=True),
        lax.psum_scatter(grad_out_weight, ("fsdp", "sp"), scatter_dimension=0, tiled=True),
        lax.psum_scatter(grad_router, ("fsdp", "sp"), scatter_dimension=0, tiled=True),
        lax.psum_scatter(grad_gain_one, ("fsdp", "sp"), scatter_dimension=0, tiled=True),
        lax.psum_scatter(grad_gain_two, ("fsdp", "sp"), scatter_dimension=0, tiled=True),
        lax.psum_scatter(grad_table, ("fsdp", "sp"), scatter_dimension=0, tiled=True),
    )
    return (
        result.astype(jnp.bfloat16),
        grad_input,
        reduced[0],
        reduced[1],
        reduced[2],
        reduced[3],
        reduced[4],
        reduced[5],
        grad_expert_in,
        grad_expert_out,
    )


def solution(mesh):
    placed = (
        P(("fsdp", "sp"), None),
        P(("fsdp", "sp"), None),
        P(("fsdp", "sp"), None),
        P(("fsdp", "sp")),
        P(),
        P(("fsdp", "sp"), None),
        P(("fsdp", "sp"), None),
        P(("fsdp", "sp"), None),
        P(("fsdp", "sp")),
        P(("fsdp", "sp")),
        P(("fsdp", "sp")),
        P(None, ("fsdp", "sp")),
        P(("fsdp", "sp"), None),
    )
    return jax.shard_map(
        body,
        mesh=mesh,
        in_specs=placed,
        out_specs=(
            P(("fsdp", "sp"), None),
            P(("fsdp", "sp"), None),
            P(("fsdp", "sp"), None),
            P(("fsdp", "sp"), None),
            P(("fsdp", "sp"), None),
            P(("fsdp", "sp")),
            P(("fsdp", "sp")),
            P(("fsdp", "sp")),
            P(None, ("fsdp", "sp")),
            P(("fsdp", "sp"), None),
        ),
        check_vma=False,
    )
```

profile of v0, /device:TPU:1, one launch (start us, length us, event | category | flops | bytes accessed | tf_op | source)
XLA Modules:
  0.0 1818.2 jit_solution(1562609553694618190)
XLA Ops:
  8.9 408.2 %gather_fusion = s32[65536]{0:T(1024)S(1)} fusion(s32[511]{0:T(512)S(1)} %copy-done.1, s32[65536]{0:T(1024)S(1)} %fusion.24), kind=kCustom, calls=%fused_computation.clone | custom fusion | bytes 786432 | tf_op jit(solution)/shard_map/while/body/eval_jaxpr/jit(_take)/gather | solution.py:84
  419.7 69.4 %all-reduce.13 = (bf16[32,12]{0,1:T(8,128)(2,1)S(1)}, bf16[768]{0:T(1024)(128)(2,1)S(1)}, bf16[768]{0:T(1024)(128)(2,1)S(1)}) all-reduce(bf16[32,12]{0,1:T(8,128)(2,1)S(1)} %copy.93, bf16[768]{0:T(1024)(128)(2,1)S(1)} %dynamic-update-slice, bf16[768]{0:T(1024)(128)(2,1)S(1)} %dynamic-update-slice.2), channel_id=1, replica_groups=mesh['fsdp'=64,'sp'=2] {'fsdp','sp'}, use_global_device_ids=true, to_apply=%add.1 | all-reduce | flops 1920 | bytes 7680
  489.4 12.6 copy.95
  506.5 6.6 reshape.277
  520.9 7.4 all-to-all-done
  539.1 310.3 %all-gather.2 = bf16[128,6,16]{2,1,0:T(8,128)(2,1)S(1)} all-gather(bf16[1,6,16]{2,1,0:T(8,128)(2,1)S(1)} %bitcast.128), channel_id=1, replica_groups=mesh['fsdp'=64,'sp'=2] {'fsdp','sp'}, dimensions={0}, use_global_device_ids=true | all-gather | bytes 24768 | tf_op jit(solution)/shard_map/all_gather | solution.py:55
  865.5 9.6 all-to-all-start.4
  875.5 41.9 %all-to-all-done.4 = bf16[128,10,768]{2,1,0:T(8,128)(2,1)} async-done(((bf16[128,10,768]{2,1,0:T(8,128)(2,1)}), bf16[128,10,768]{2,1,0:T(8,128)(2,1)}, u32[]{:S(2)}, u32[]{:S(2)}) %all-to-all-start.4) | async-done | bytes 1966112 | tf_op jit(solution)/shard_map/all_to_all | solution.py:178
  924.3 4.9 reshape.229
  933.3 33.3 %all-to-all-done.2 = bf16[128,10,768]{2,1,0:T(8,128)(2,1)} async-done(((bf16[128,10,768]{2,1,0:T(8,128)(2,1)}), bf16[128,10,768]{2,1,0:T(8,128)(2,1)}, u32[]{:S(2)}, u32[]{:S(2)}) %all-to-all-start.2) | async-done | bytes 1966112 | tf_op jit(solution)/shard_map/all_to_all | solution.py:133
  971.4 5.6 fusion.8
  999.2 33.2 %all-to-all-done.5 = bf16[128,10,768]{2,1,0:T(8,128)(2,1)} async-done(((bf16[128,10,768]{2,1,0:T(8,128)(2,1)}), bf16[128,10,768]{2,1,0:T(8,128)(2,1)}, u32[]{:S(2)}, u32[]{:S(2)}) %all-to-all-start.5) | async-done | bytes 1966112 | tf_op jit(solution)/shard_map/all_to_all | solution.py:194
  1032.4 5.3 all-to-all-start.3
  1042.4 37.5 %all-to-all-done.3 = bf16[128,10,768]{2,1,0:T(8,128)(2,1)} async-done(((bf16[128,10,768]{2,1,0:T(8,128)(2,1)}), bf16[128,10,768]{2,1,0:T(8,128)(2,1)}, u32[]{:S(2)}, u32[]{:S(2)}) %all-to-all-start.3) | async-done | bytes 1966112 | tf_op jit(solution)/shard_map/all_to_all | solution.py:140
  1116.1 8.2 all-to-all-done.7
  1128.5 5.1 fusion.34
  1133.5 357.1 %fusion.52 = (f32[8,2304]{1,0:T(8,128)}, f32[8,768]{1,0:T(8,128)}) fusion(f32[768,2304]{1,0:T(8,128)} %fusion.34, f32[768,768]{1,0:T(8,128)S(1)} %fusion.28), kind=kCustom, calls=%all-reduce-scatter.2 | all-reduce-scatter fusion | flops 3145729 | bytes 9535488
  1497.0 6.9 collective-permute-start.63
  1514.0 14.1 collective-permute-start.54
  1568.5 5.4 collective-permute-start.38
  1647.2 66.7 %all-reduce.12 = (f32[768,16]{1,0:T(8,128)S(1)}, f32[768]{0:T(1024)S(1)}, f32[768]{0:T(1024)S(1)}, f32[384]{0:T(512)S(1)}) all-reduce(f32[768,16]{1,0:T(8,128)S(1)} %fusion.50, f32[768]{0:T(1024)S(1)} %get-tuple-element.67, f32[768]{0:T(1024)S(1)} %copy-done.81, f32[384]{0:T(512)} %reshape.238), channel_id=4, replica_groups=mesh['fsdp'=64,'sp'=2] {'fsdp','sp'}, use_global_device_ids=true, to_apply=%region_17.20.clone | all-reduce | flops 14208 | bytes 113664
  1735.8 27.2 %concatenate.1 = f32[262,768]{1,0:T(8,128)S(1)} concatenate(f32[6,768]{1,0:T(8,128)} %copy-done.62, f32[8,768]{1,0:T(8,128)} %collective-permute-done.62, f32[8,768]{1,0:T(8,128)} %collective-permute-done.61, f32[8,768]{1,0:T(8,128)} %collective-permute-done.60, f32[8,768]{1,0:T(8,128)} %collective-permute-done.59, f32[8,768]{1,0:T(8,128)} %collective-permute-done.58, ...), dimensions={0} | concatenate | bytes 1609728
  1765.1 6.4 collective-permute-start.3
  1783.0 27.3 %concatenate = f32[262,2304]{1,0:T(8,128)S(1)} concatenate(f32[6,2304]{1,0:T(8,128)} %copy-done.29, f32[8,2304]{1,0:T(8,128)} %copy-done.28, f32[8,2304]{1,0:T(8,128)S(1)} %copy-done.31, f32[8,2304]{1,0:T(8,128)S(1)} %copy-done.33, f32[8,2304]{1,0:T(8,128)S(1)} %copy-done.35, f32[8,2304]{1,0:T(8,128)} %copy-done.36, f32[8,2304]{1,0:T(8,128)S(1)} %copy-done.38, ...), dimensions={0} | concatenate | bytes 4829184
  (468 shorter events, 290.8 us)
Async XLA Ops:
  7.2 499.3 %all-gather.6.cloned.1.call-start = ((), (), s32[]{:S(2)}) async-start(), calls=%async_computation.8 | async-start | bytes 4755456 | tf_op jit(solution)/shard_map/all_gather | solution.py:53
  7.9 842.2 %all-gather.8.cloned.1.call-start = ((), (), s32[]{:S(2)}) async-start(), calls=%async_computation.9 | async-start | bytes 1585152 | tf_op jit(solution)/shard_map/all_gather | solution.py:54
  534.4 318.1 %all-to-all-start.1 = ((bf16[2,2,24576]{2,1,0:T(2,128)(2,1)}), bf16[2,2,24576]{2,1,0:T(2,128)(2,1)}, u32[]{:S(2)}, u32[]{:S(2)}) async-start(bf16[2,2,24576]{2,1,0:T(2,128)(2,1)} %reshape.290), calls=%async_computation.1 | async-start | bytes 393216 | tf_op jit(solution)/shard_map/all_to_all | solution.py:110
  865.5 51.9 %all-to-all-start.4 = ((bf16[128,10,768]{2,1,0:T(8,128)(2,1)}), bf16[128,10,768]{2,1,0:T(8,128)(2,1)}, u32[]{:S(2)}, u32[]{:S(2)}) async-start(bf16[128,10,768]{2,1,0:T(8,128)(2,1)} %bitcast.104), calls=%async_computation.4 | async-start | bytes 6291456 | tf_op jit(solution)/shard_map/all_to_all | solution.py:178
  919.3 47.2 %all-to-all-start.2 = ((bf16[128,10,768]{2,1,0:T(8,128)(2,1)}), bf16[128,10,768]{2,1,0:T(8,128)(2,1)}, u32[]{:S(2)}, u32[]{:S(2)}) async-start(bf16[128,10,768]{2,1,0:T(8,128)(2,1)} %bitcast.105), calls=%async_computation.2 | async-start | bytes 6291456 | tf_op jit(solution)/shard_map/all_to_all | solution.py:133
  985.2 47.2 %all-to-all-start.5 = ((bf16[128,10,768]{2,1,0:T(8,128)(2,1)}), bf16[128,10,768]{2,1,0:T(8,128)(2,1)}, u32[]{:S(2)}, u32[]{:S(2)}) async-start(bf16[128,10,768]{2,1,0:T(8,128)(2,1)} %reshape.230), calls=%async_computation.5 | async-start | bytes 6291456 | tf_op jit(solution)/shard_map/all_to_all | solution.py:194
  1032.4 47.4 %all-to-all-start.3 = ((bf16[128,10,768]{2,1,0:T(8,128)(2,1)}), bf16[128,10,768]{2,1,0:T(8,128)(2,1)}, u32[]{:S(2)}, u32[]{:S(2)}) async-start(bf16[128,10,768]{2,1,0:T(8,128)(2,1)} %reshape.224), calls=%async_computation.3 | async-start | bytes 6291456 | tf_op jit(solution)/shard_map/all_to_all | solution.py:140
  1506.4 21.6 %collective-permute-start.58 = (f32[8,768]{1,0:T(8,128)}, f32[8,768]{1,0:T(8,128)}, u32[]{:S(2)}, u32[]{:S(2)}) collective-permute-start(f32[8,768]{1,0:T(8,128)} %get-tuple-element.92), channel_id=1, source_target_pairs={{0,27},{1,28},{2,29},{3,30},{4,31},{5,32},{6,33},{7,34},{8,35},{9,... | collective-permute-start | bytes 73736
  1508.3 22.2 %collective-permute-start.57 = (f32[8,768]{1,0:T(8,128)}, f32[8,768]{1,0:T(8,128)}, u32[]{:S(2)}, u32[]{:S(2)}) collective-permute-start(f32[8,768]{1,0:T(8,128)} %get-tuple-element.92), channel_id=1, source_target_pairs={{0,26},{1,27},{2,28},{3,29},{4,30},{5,31},{6,32},{7,33},{8,34},{9,... | collective-permute-start | bytes 73736
  1510.2 22.2 %collective-permute-start.56 = (f32[8,768]{1,0:T(8,128)}, f32[8,768]{1,0:T(8,128)}, u32[]{:S(2)}, u32[]{:S(2)}) collective-permute-start(f32[8,768]{1,0:T(8,128)} %get-tuple-element.92), channel_id=1, source_target_pairs={{0,25},{1,26},{2,27},{3,28},{4,29},{5,30},{6,31},{7,32},{8,33},{9,... | collective-permute-start | bytes 73736
  1512.1 22.2 %collective-permute-start.55 = (f32[8,768]{1,0:T(8,128)}, f32[8,768]{1,0:T(8,128)}, u32[]{:S(2)}, u32[]{:S(2)}) collective-permute-start(f32[8,768]{1,0:T(8,128)} %get-tuple-element.92), channel_id=1, source_target_pairs={{0,24},{1,25},{2,26},{3,27},{4,28},{5,29},{6,30},{7,31},{8,32},{9,... | collective-permute-start | bytes 73736
  1514.0 22.4 %collective-permute-start.54 = (f32[8,768]{1,0:T(8,128)}, f32[8,768]{1,0:T(8,128)}, u32[]{:S(2)}, u32[]{:S(2)}) collective-permute-start(f32[8,768]{1,0:T(8,128)} %get-tuple-element.92), channel_id=1, source_target_pairs={{0,23},{1,24},{2,25},{3,26},{4,27},{5,28},{6,29},{7,30},{8,31},{9,... | collective-permute-start | bytes 73736
  1552.3 21.5 %collective-permute-start.42 = (f32[8,768]{1,0:T(8,128)}, f32[8,768]{1,0:T(8,128)S(1)}, u32[]{:S(2)}, u32[]{:S(2)}) collective-permute-start(f32[8,768]{1,0:T(8,128)} %get-tuple-element.92), channel_id=1, source_target_pairs={{0,11},{1,12},{2,13},{3,14},{4,15},{5,16},{6,17},{7,18},{8,19},{9,... | collective-permute-start | bytes 73736
  1555.8 20.9 %collective-permute-start.41 = (f32[8,768]{1,0:T(8,128)}, f32[8,768]{1,0:T(8,128)S(1)}, u32[]{:S(2)}, u32[]{:S(2)}) collective-permute-start(f32[8,768]{1,0:T(8,128)} %get-tuple-element.92), channel_id=1, source_target_pairs={{0,10},{1,11},{2,12},{3,13},{4,14},{5,15},{6,16},{7,17},{8,18},{9,... | collective-permute-start | bytes 73736
  1634.4 81.3 %collective-permute-start.14 = (f32[8,2304]{1,0:T(8,128)S(1)}, f32[8,2304]{1,0:T(8,128)S(1)}, u32[]{:S(2)}, u32[]{:S(2)}) collective-permute-start(f32[8,2304]{1,0:T(8,128)S(1)} %copy-done.23), channel_id=1, source_target_pairs={{0,15},{1,16},{2,17},{3,18},{4,19},{5,20},{6,21},{7,22},{8,23},{9,... | collective-permute-start | bytes 221192
  1636.5 81.8 %collective-permute-start.13 = (f32[8,2304]{1,0:T(8,128)S(1)}, f32[8,2304]{1,0:T(8,128)S(1)}, u32[]{:S(2)}, u32[]{:S(2)}) collective-permute-start(f32[8,2304]{1,0:T(8,128)S(1)} %copy-done.23), channel_id=1, source_target_pairs={{0,14},{1,15},{2,16},{3,17},{4,18},{5,19},{6,20},{7,21},{8,22},{9,... | collective-permute-start | bytes 221192
  1639.1 83.7 %collective-permute-start.12 = (f32[8,2304]{1,0:T(8,128)S(1)}, f32[8,2304]{1,0:T(8,128)S(1)}, u32[]{:S(2)}, u32[]{:S(2)}) collective-permute-start(f32[8,2304]{1,0:T(8,128)S(1)} %copy-done.23), channel_id=1, source_target_pairs={{0,13},{1,14},{2,15},{3,16},{4,17},{5,18},{6,19},{7,20},{8,21},{9,... | collective-permute-start | bytes 221192
  1640.9 85.9 %collective-permute-start.11 = (f32[8,2304]{1,0:T(8,128)S(1)}, f32[8,2304]{1,0:T(8,128)S(1)}, u32[]{:S(2)}, u32[]{:S(2)}) collective-permute-start(f32[8,2304]{1,0:T(8,128)S(1)} %copy-done.23), channel_id=1, source_target_pairs={{0,12},{1,13},{2,14},{3,15},{4,16},{5,17},{6,18},{7,19},{8,20},{9,... | collective-permute-start | bytes 221192
  1643.2 88.0 %collective-permute-start.10 = (f32[8,2304]{1,0:T(8,128)S(1)}, f32[8,2304]{1,0:T(8,128)S(1)}, u32[]{:S(2)}, u32[]{:S(2)}) collective-permute-start(f32[8,2304]{1,0:T(8,128)S(1)} %copy-done.23), channel_id=1, source_target_pairs={{0,11},{1,12},{2,13},{3,14},{4,15},{5,16},{6,17},{7,18},{8,19},{9,... | collective-permute-start | bytes 221192
  1715.7 47.4 %collective-permute-start.9 = (f32[8,2304]{1,0:T(8,128)S(1)}, f32[8,2304]{1,0:T(8,128)S(1)}, u32[]{:S(2)}, u32[]{:S(2)}) collective-permute-start(f32[8,2304]{1,0:T(8,128)S(1)} %copy-done.23), channel_id=1, source_target_pairs={{0,10},{1,11},{2,12},{3,13},{4,14},{5,15},{6,16},{7,17},{8,18},{9,... | collective-permute-start | bytes 221192
  1718.3 46.8 %collective-permute-start.8 = (f32[8,2304]{1,0:T(8,128)S(1)}, f32[8,2304]{1,0:T(8,128)S(1)}, u32[]{:S(2)}, u32[]{:S(2)}) collective-permute-start(f32[8,2304]{1,0:T(8,128)S(1)} %copy-done.23), channel_id=1, source_target_pairs={{0,9},{1,10},{2,11},{3,12},{4,13},{5,14},{6,15},{7,16},{8,17},{9,1... | collective-permute-start | bytes 221192
  1722.8 48.8 %collective-permute-start.7 = (f32[8,2304]{1,0:T(8,128)S(1)}, f32[8,2304]{1,0:T(8,128)S(1)}, u32[]{:S(2)}, u32[]{:S(2)}) collective-permute-start(f32[8,2304]{1,0:T(8,128)S(1)} %copy-done.23), channel_id=1, source_target_pairs={{0,8},{1,9},{2,10},{3,11},{4,12},{5,13},{6,14},{7,15},{8,16},{9,17... | collective-permute-start | bytes 221192
  1726.8 48.4 %collective-permute-start.6 = (f32[8,2304]{1,0:T(8,128)S(1)}, f32[8,2304]{1,0:T(8,128)S(1)}, u32[]{:S(2)}, u32[]{:S(2)}) collective-permute-start(f32[8,2304]{1,0:T(8,128)S(1)} %copy-done.23), channel_id=1, source_target_pairs={{0,7},{1,8},{2,9},{3,10},{4,11},{5,12},{6,13},{7,14},{8,15},{9,16}... | collective-permute-start | bytes 221192
  1731.1 46.0 %collective-permute-start.5 = (f32[8,2304]{1,0:T(8,128)S(1)}, f32[8,2304]{1,0:T(8,128)S(1)}, u32[]{:S(2)}, u32[]{:S(2)}) collective-permute-start(f32[8,2304]{1,0:T(8,128)S(1)} %copy-done.23), channel_id=1, source_target_pairs={{0,6},{1,7},{2,8},{3,9},{4,10},{5,11},{6,12},{7,13},{8,14},{9,15},... | collective-permute-start | bytes 221192
  (159 other events, 4735.7 us)
Sparse Core Ops, SparseCore 0:
  9.7 312.3 all-gather.5
  323.9 300.4 all-gather.7
where the time goes:
time: 1830 us; the launch traced here: 1820 us
  blocking collectives  803 us (44%)
  local copies, waits for them, and re-layouts  543 us (30%)
  starting transfers between devices  217 us (12%)
  waiting for transfers between devices  168 us (9%)
  matrix products  50.7 us (3%)
  other arithmetic  19 us (1%)
    unnamed x3, blocking collectives  493 us
    gather x1, local copies, waits for them, and re-layouts, bucket_block(): picked = jnp.take(buckets, relative, axis=0).reshape(block_rows, length)  408 us
    all_gather x1, blocking collectives, body(): lax.all_gather(router_weight, ('fsdp', 'sp'), axis=0, tiled=True)  310 us
    unnamed x64, starting transfers between devices  177 us
    unnamed x242, local copies, waits for them, and re-layouts  79.3 us
    all_to_all x1, waiting for transfers between devices, body(): lax.all_to_all(grad_slots, ('fsdp', 'sp'), split_axis=0, concat_axis=0, t...  41.9 us
    all_to_all x1, waiting for transfers between devices, body(): lax.all_to_all(part_rows.reshape(arrived_rows.shape), ('fsdp', 'sp'), spl...  37.5 us
  transfers between devices with their start and end apart: 74, of which 8 were waited for; matrix products, arithmetic and copies ran while one was open for 28% of the time, Pallas kernels for 0%

commit v1 on v0

v1 whole, which is shorter than its diff:
```python
import functools

import jax
import jax.numpy as jnp
import numpy as np
from jax import lax
from jax.experimental import pallas as pl
from jax.experimental.pallas import tpu as pltpu
from jax.sharding import PartitionSpec as P

HEADS = 12
HEAD_DIM = 64
EXPERTS = 16
BUCKETS = 32
CAP = 10
EPSILON = 1e-06
MESH = pl.DeviceIdType.MESH
BF = jnp.bfloat16
F32 = jnp.float32
ANY = pl.BlockSpec(memory_space=pl.ANY)
SLOT = 24
GELU_C = 0.7978845608028654
GELU_A = 0.044715


def flat_id():
    return lax.axis_index("fsdp") * 2 + lax.axis_index("sp")


def coords(flat):
    return (lax.div(flat, 2), lax.rem(flat, 2))


QUAD = (4, lambda f: lax.rem(f, 4), lambda f, k: f - lax.rem(f, 4) + k)
SAME_M = (32, lambda f: lax.div(f, 4), lambda f, k: 4 * k + lax.rem(f, 4))
SAME_R = (16, lambda f: lax.div(f, 8), lambda f, k: 8 * k + lax.rem(f, 8))
PLANE = (
    4,
    lambda f: lax.div(lax.rem(f, 8), 4) * 2 + lax.rem(f, 2),
    lambda f, k: lax.div(f, 8) * 8
    + lax.div(k, 2) * 4
    + lax.rem(lax.div(f, 2), 2) * 2
    + lax.rem(k, 2),
)
MATE = (
    2,
    lambda f: lax.rem(lax.div(f, 2), 2),
    lambda f, k: f - lax.rem(lax.div(f, 2), 2) * 2 + 2 * k,
)


def for_range(low, high, fn):
    if high - low <= 4:
        for j in range(low, high):
            fn(j)
    else:

        def step(j, carry):
            fn(j)
            return carry

        lax.fori_loop(low, high, step, 0)


def greet(f, group):
    size, pos, peer = group
    me = pos(f)
    barrier = pltpu.get_barrier_semaphore()

    def hello(j):
        pl.semaphore_signal(
            barrier,
            inc=1,
            device_id=coords(peer(f, lax.rem(me + j, size))),
            device_id_type=MESH,
        )

    for_range(1, size, hello)
    pl.semaphore_wait(barrier, size - 1)


def exchange_kernel(group, kinds, *refs):
    count = len(kinds)
    ins, outs = refs[:count], refs[count : 2 * count]
    send, recv, own = refs[2 * count :]
    size, pos, peer = group
    f = flat_id()
    me = pos(f)
    greet(f, group)

    def copy(a, j):
        p = lax.rem(me + j, size)
        return pltpu.make_async_remote_copy(
            src_ref=ins[a] if kinds[a] else ins[a].at[p],
            dst_ref=outs[a].at[me],
            send_sem=send.at[a, j],
            recv_sem=recv.at[a, j],
            device_id=coords(peer(f, p)),
            device_id_type=MESH,
        )

    def local(a):
        return pltpu.make_async_copy(
            ins[a] if kinds[a] else ins[a].at[me], outs[a].at[me], own.at[a]
        )

    def start(j):
        for a in range(count):
            copy(a, j).start()

    def wait(j):
        for a in range(count):
            copy(a, j).wait()

    for_range(1, size, start)
    for a in range(count):
        local(a).start()
    for a in range(count):
        local(a).wait()
    for_range(1, size, wait)


def exchange(cid, group, *items):
    size = group[0]
    arrays = [array for array, gather in items]
    kinds = tuple(gather for array, gather in items)
    out = [
        jax.ShapeDtypeStruct((size,) + (a.shape if k else a.shape[1:]), a.dtype)
        for a, k in zip(arrays, kinds)
    ]
    moved = sum(a.size * a.dtype.itemsize * (size if k else 1) for a, k in zip(arrays, kinds))
    return pl.pallas_call(
        functools.partial(exchange_kernel, group, kinds),
        out_shape=out,
        in_specs=[ANY] * len(arrays),
        out_specs=[ANY] * len(arrays),
        scratch_shapes=[
            pltpu.SemaphoreType.DMA((len(arrays), size)),
            pltpu.SemaphoreType.DMA((len(arrays), size)),
            pltpu.SemaphoreType.DMA((len(arrays),)),
        ],
        compiler_params=pltpu.CompilerParams(collective_id=cid, has_side_effects=True),
        cost_estimate=pl.CostEstimate(flops=0, bytes_accessed=2 * moved, transcendentals=0),
    )(*arrays)


def weights_kernel(a_in, b_in, a_out, b_out, send_a, recv_a, send_b, recv_b, own):
    f = flat_id()
    m, g = lax.rem(f, 4), lax.div(f, 4)
    plane, place = lax.div(g, 8), lax.rem(g, 8)
    greet(f, SAME_M)

    def copy_a(j):
        return pltpu.make_async_remote_copy(
            src_ref=a_in,
            dst_ref=a_out.at[g],
            send_sem=send_a.at[j],
            recv_sem=recv_a.at[j],
            device_id=coords(4 * lax.rem(g + j, 32) + m),
            device_id_type=MESH,
        )

    def copy_b(j, q):
        return pltpu.make_async_remote_copy(
            src_ref=b_in,
            dst_ref=b_out.at[q],
            send_sem=send_b.at[j],
            recv_sem=recv_b.at[q],
            device_id=coords(4 * lax.rem(g + j, 32) + m),
            device_id_type=MESH,
        )

    for_range(1, 32, lambda j: copy_a(j).start())
    mine_a = pltpu.make_async_copy(a_in, a_out.at[g], own.at[0])
    mine_a.start()

    @pl.when(plane == m)
    def _():
        for_range(1, 32, lambda j: copy_b(j, place).start())
        mine_b = pltpu.make_async_copy(b_in, b_out.at[place], own.at[1])
        mine_b.start()
        mine_b.wait()

    mine_a.wait()
    for_range(1, 32, lambda j: copy_a(j).wait())

    def take(q):
        @pl.when(8 * m + q != g)
        def _():
            copy_b(1, q).wait_recv()

    for_range(0, 8, take)

    @pl.when(plane == m)
    def _():
        for_range(1, 32, lambda j: copy_b(j, place).wait_send())


def gather_weights(cid, a, b):
    return pl.pallas_call(
        weights_kernel,
        out_shape=[
            jax.ShapeDtypeStruct((32,) + a.shape, a.dtype),
            jax.ShapeDtypeStruct((8,) + b.shape, b.dtype),
        ],
        in_specs=[ANY] * 2,
        out_specs=[ANY] * 2,
        scratch_shapes=[
            pltpu.SemaphoreType.DMA((32,)),
            pltpu.SemaphoreType.DMA((32,)),
            pltpu.SemaphoreType.DMA((32,)),
            pltpu.SemaphoreType.DMA((8,)),
            pltpu.SemaphoreType.DMA((2,)),
        ],
        compiler_params=pltpu.CompilerParams(collective_id=cid, has_side_effects=True),
    )(a, b)


def grads_kernel(a_in, b_in, a_out, b_out, send_a, recv_a, send_b, recv_b, own):
    f = flat_id()
    m, g = lax.rem(f, 4), lax.div(f, 4)
    plane, place = lax.div(g, 8), lax.rem(g, 8)
    greet(f, SAME_M)

    def copy_a(j):
        p = lax.rem(g + j, 32)
        return pltpu.make_async_remote_copy(
            src_ref=a_in.at[p],
            dst_ref=a_out.at[g],
            send_sem=send_a.at[j],
            recv_sem=recv_a.at[j],
            device_id=coords(4 * p + m),
            device_id_type=MESH,
        )

    def copy_b(q):
        p = 8 * m + q
        return pltpu.make_async_remote_copy(
            src_ref=b_in.at[q],
            dst_ref=b_out.at[g],
            send_sem=send_b.at[q],
            recv_sem=recv_b.at[lax.rem(p - g + 32, 32)],
            device_id=coords(4 * p + m),
            device_id_type=MESH,
        )

    def away(q, fn):
        @pl.when(8 * m + q != g)
        def _():
            fn(q)

    for_range(0, 8, lambda q: away(q, lambda k: copy_b(k).start()))
    for_range(1, 32, lambda j: copy_a(j).start())
    mine_a = pltpu.make_async_copy(a_in.at[g], a_out.at[g], own.at[0])
    mine_a.start()

    @pl.when(plane == m)
    def _():
        mine_b = pltpu.make_async_copy(b_in.at[place], b_out.at[g], own.at[1])
        mine_b.start()
        mine_b.wait()

    mine_a.wait()
    for_range(1, 32, lambda j: copy_a(j).wait())
    for_range(0, 8, lambda q: away(q, lambda k: copy_b(k).wait_send()))

    @pl.when(plane == m)
    def _():
        def take(j):
            sender = lax.rem(g - j + 32, 32)
            pltpu.make_async_remote_copy(
                src_ref=b_in.at[0],
                dst_ref=b_out.at[sender],
                send_sem=send_b.at[0],
                recv_sem=recv_b.at[j],
                device_id=coords(4 * sender + m),
                device_id_type=MESH,
            ).wait_recv()

        for_range(1, 32, take)


def scatter_grads(cid, a, b):
    return pl.pallas_call(
        grads_kernel,
        out_shape=[
            jax.ShapeDtypeStruct(a.shape, a.dtype),
            jax.ShapeDtypeStruct((32,) + b.shape[1:], b.dtype),
        ],
        in_specs=[ANY] * 2,
        out_specs=[ANY] * 2,
        scratch_shapes=[
            pltpu.SemaphoreType.DMA((32,)),
            pltpu.SemaphoreType.DMA((32,)),
            pltpu.SemaphoreType.DMA((8,)),
            pltpu.SemaphoreType.DMA((32,)),
            pltpu.SemaphoreType.DMA((2,)),
        ],
        compiler_params=pltpu.CompilerParams(collective_id=cid, has_side_effects=True),
    )(a, b)


def compute(kernel, out, *args, flops=0):
    return pl.pallas_call(
        kernel,
        out_shape=out,
        compiler_params=pltpu.CompilerParams(vmem_limit_bytes=48 * 1024 * 1024),
        cost_estimate=pl.CostEstimate(
            flops=flops,
            bytes_accessed=sum(a.size * a.dtype.itemsize for a in args),
            transcendentals=0,
        ),
    )(*args)


def dot(a, b, dims=((1,), (0,)), precision=None):
    return lax.dot_general(
        a, b, (dims, ((), ())), precision=precision, preferred_element_type=F32
    )


def rms_scale(values):
    return lax.rsqrt(jnp.mean(values * values, axis=-1, keepdims=True) + EPSILON)


def rms_back(grad, values, scale, gain):
    weighted = grad * gain
    inner = jnp.mean(weighted * values, axis=-1, keepdims=True)
    return scale * weighted - values * (scale * scale * scale * inner)


def bucket_hot(buckets):
    return (lax.broadcasted_iota(jnp.int32, (BUCKETS, 512), 0) == buckets).astype(F32)


def attend_kernel(x, w, b, gain, table, buckets, normed_o, proj_o, probs_o, mixed_o, part_o):
    values = x[...].astype(F32).reshape(512, 768)
    normed = (values * rms_scale(values) * gain[...]).astype(BF)
    normed_o[...] = normed
    proj = dot(normed, w[:, :576]).astype(BF)
    proj_o[...] = proj
    by_offset = dot(table[...], bucket_hot(buckets[...]).astype(BF))
    seqs = [[], []]
    for h in range(3):
        line = jnp.broadcast_to(by_offset[h : h + 1], (256, 512))
        bias = pltpu.roll(line, 257, 1, stride=1, stride_axis=0)[:, :256]
        for s in range(2):
            rows = slice(256 * s, 256 * s + 256)
            query = proj[rows, 64 * h : 64 * h + 64]
            key = proj[rows, 192 + 64 * h : 256 + 64 * h]
            value = proj[rows, 384 + 64 * h : 448 + 64 * h]
            scores = dot(query, key, ((1,), (1,))) + bias
            exponent = jnp.exp(scores - jnp.max(scores, axis=-1, keepdims=True))
            probs = exponent / jnp.sum(exponent, axis=-1, keepdims=True)
            probs_o[3 * s + h] = probs
            seqs[s].append(dot(probs.astype(BF), value).astype(BF))
    mixed = jnp.concatenate([jnp.concatenate(s, axis=1) for s in seqs], axis=0)
    mixed_o[...] = mixed
    part_o[...] = dot(mixed, b[...]).astype(BF).reshape(4, 128, 768)


def route_kernel(
    x, parts, gain, router, routes, drop, cot, after_o, normed_o, probs_o, pick_o, send_o
):
    after = x[...].astype(F32) + jnp.sum(parts[...].astype(F32), axis=0)
    after_o[...] = after
    normed = (after * rms_scale(after) * gain[...]).astype(BF)
    normed_o[...] = normed
    logits = dot(normed, router[...])
    exponent = jnp.exp(logits - jnp.max(logits, axis=-1, keepdims=True))
    probs = exponent / jnp.sum(exponent, axis=-1, keepdims=True)
    probs_o[...] = probs
    chosen = routes[...]
    hot = chosen == lax.broadcasted_iota(jnp.int32, (128, EXPERTS), 1)
    gates = jnp.sum(jnp.where(hot, probs, 0.0), axis=-1, keepdims=True)
    kept = drop[...].astype(F32)
    grad_y = (cot[...].astype(F32) * (kept * gates)).astype(BF)
    earlier = lax.broadcasted_iota(jnp.int32, (128, 128), 1) < lax.broadcasted_iota(
        jnp.int32, (128, 128), 0
    )
    counts = dot(earlier.astype(F32).astype(BF), hot.astype(F32).astype(BF))
    slot = jnp.sum(jnp.where(hot, counts, 0.0), axis=-1, keepdims=True).astype(jnp.int32)
    place = jnp.where(drop[...] > 0, chosen * SLOT + slot, -SLOT)
    lanes = lax.broadcasted_iota(jnp.int32, (128, EXPERTS * SLOT), 1)
    pick = jnp.concatenate(
        [(lanes == place).astype(F32), (lanes == place + CAP).astype(F32)], axis=0
    ).astype(BF)
    pick_o[...] = pick
    both = jnp.concatenate([normed, grad_y], axis=0)
    send_o[...] = dot(pick, both, ((0,), (0,))).astype(BF).reshape(EXPERTS, SLOT, 768)


def compact_kernel(choose, x, out):
    flat = x[...].astype(F32).reshape(EXPERTS * SLOT, 768).astype(BF)
    out[...] = dot(choose[...], flat).astype(BF)


def expand_kernel(choose, x, out):
    total = jnp.sum(x[...].astype(F32), axis=0).astype(BF)
    out[...] = dot(choose[...], total, ((0,), (0,))).astype(BF).reshape(EXPERTS, SLOT, 768)


def add_kernel(x, out):
    out[...] = (x[0].astype(F32) + x[1].astype(F32)).astype(BF)


def expert_kernel(rows, w_in, w_out, parts, grad_in, grad_out):
    @pl.when(pl.program_id(0) == 0)
    def _():
        grad_in[...] = jnp.zeros_like(grad_in)
        grad_out[...] = jnp.zeros_like(grad_out)

    row = rows[:, 0].reshape(320, 768)
    grad = rows[:, 1].reshape(320, 768)
    pre = dot(row, w_in[...])
    square = pre * pre
    tanh = jnp.tanh(GELU_C * (pre + GELU_A * (pre * square)))
    half = 0.5 * (1.0 + tanh)
    act = (pre * half).astype(BF)
    slope = half + (0.5 * GELU_C) * pre * (1.0 - tanh * tanh) * (1.0 + 3.0 * GELU_A * square)
    parts[:, 0] = dot(act, w_out[...]).astype(BF).reshape(2, 160, 768)
    grad_act = dot(grad, w_out[...], ((1,), (1,)))
    grad_pre = (grad_act * slope).astype(BF)
    parts[:, 1] = dot(grad_pre, w_in[...], ((1,), (1,))).astype(BF).reshape(2, 160, 768)
    grad_in[...] += dot(row, grad_pre, ((0,), (0,)))
    grad_out[...] += dot(act, grad, ((0,), (0,)))


def experts(rows, w_in, w_out):
    block = pl.BlockSpec((2, 2, 160, 768), lambda i: (i, 0, 0, 0))
    whole_in = pl.BlockSpec((768, 384), lambda i: (0, 0))
    whole_out = pl.BlockSpec((384, 768), lambda i: (0, 0))
    return pl.pallas_call(
        expert_kernel,
        grid=(4,),
        out_shape=[
            jax.ShapeDtypeStruct((8, 2, 160, 768), BF),
            jax.ShapeDtypeStruct((768, 384), F32),
            jax.ShapeDtypeStruct((384, 768), F32),
        ],
        in_specs=[block, whole_in, whole_out],
        out_specs=[block, whole_in, whole_out],
        compiler_params=pltpu.CompilerParams(vmem_limit_bytes=48 * 1024 * 1024),
        cost_estimate=pl.CostEstimate(
            flops=12 * 1280 * 768 * 384, bytes_accessed=12000000, transcendentals=0
        ),
    )(rows, w_in, w_out)


def after_kernel(
    back,
    pick,
    after,
    normed,
    probs,
    routes,
    drop,
    cot,
    gain,
    router,
    result_o,
    grad_after_o,
    grad_low_o,
    grad_router_o,
    grad_gain_o,
):
    flat = back[...].astype(F32).reshape(EXPERTS * SLOT, 768).astype(BF)
    expert_y = dot(pick[:128], flat)
    slot_grad = dot(pick[128:], flat)
    hot = routes[...] == lax.broadcasted_iota(jnp.int32, (128, EXPERTS), 1)
    gates = jnp.sum(jnp.where(hot, probs[...], 0.0), axis=-1, keepdims=True)
    kept = drop[...].astype(F32)
    values = after[...]
    result_o[...] = (values + (kept * gates) * expert_y).astype(BF)
    grad = cot[...].astype(F32)
    grad_gate = kept * jnp.sum(grad * expert_y, axis=-1, keepdims=True)
    grad_logits = ((grad_gate * gates) * (hot.astype(F32) - probs[...])).astype(BF)
    grad_router_o[...] = dot(normed[...], grad_logits, ((0,), (0,)))
    grad_normed = dot(grad_logits, router[...], ((1,), (1,))) + slot_grad
    scale = rms_scale(values)
    grad_gain_o[...] = jnp.sum(grad_normed * values * scale, axis=0, keepdims=True)
    grad_after = grad + rms_back(grad_normed, values, scale, gain[...])
    grad_after_o[...] = grad_after
    grad_low_o[...] = grad_after.astype(BF)


def attend_back_kernel(
    x,
    normed,
    proj,
    probs,
    mixed,
    grad_proj,
    w,
    b,
    buckets,
    grad_qkv_o,
    grad_out_o,
    part_o,
    grad_gain_o,
    grad_table_o,
):
    values = x[...].astype(F32).reshape(512, 768)
    grad_in = grad_proj[...].reshape(512, 768)
    grad_mixed = dot(grad_in, b[...], ((1,), (1,))).astype(BF)
    grad_out_o[...] = dot(mixed[...], grad_in, ((0,), (0,))).astype(BF).reshape(8, 24, 768)
    flip = (
        lax.broadcasted_iota(jnp.int32, (256, 256), 0)
        + lax.broadcasted_iota(jnp.int32, (256, 256), 1)
        == 255
    )
    flip = flip.astype(F32).astype(BF)
    pieces = [[[], [], []], [[], [], []]]
    sums = []
    for h in range(3):
        turned = jnp.zeros((256, 256), F32)
        for s in range(2):
            rows = slice(256 * s, 256 * s + 256)
            query = proj[rows, 64 * h : 64 * h + 64]
            key = proj[rows, 192 + 64 * h : 256 + 64 * h]
            value = proj[rows, 384 + 64 * h : 448 + 64 * h]
            grad_rows = grad_mixed[rows, 64 * h : 64 * h + 64]
            weights = probs[3 * s + h]
            grad_probs = dot(grad_rows, value, ((1,), (1,)))
            inner = jnp.sum(weights * grad_probs, axis=-1, keepdims=True)
            grad_scores = (weights * (grad_probs - inner)).astype(BF)
            turned = turned + dot(flip, grad_scores)
            pieces[s][0].append(dot(grad_scores, key).astype(BF))
            pieces[s][1].append(dot(grad_scores, query, ((0,), (0,))).astype(BF))
            pieces[s][2].append(dot(weights.astype(BF), grad_rows, ((0,), (0,))).astype(BF))
        wide = jnp.concatenate([turned, jnp.zeros((256, 256), F32)], axis=1)
        wide = pltpu.roll(wide, 0, 1, stride=1, stride_axis=0)
        sums.append(jnp.sum(wide, axis=0, keepdims=True))
    sums = jnp.concatenate(sums + [jnp.zeros((5, 512), F32)], axis=0)
    grad_table_o[...] = dot(
        sums, bucket_hot(buckets[...]), ((1,), (1,)), precision=lax.Precision.HIGHEST
    )
    grad_qkv = jnp.concatenate(
        [jnp.concatenate([p for part in s for p in part], axis=1) for s in pieces], axis=0
    )
    grad_qkv_o[...] = dot(normed[...], grad_qkv, ((0,), (0,)))
    grad_normed = dot(grad_qkv, w[:, :576], ((1,), (1,)))
    part_o[...] = grad_normed.astype(BF).reshape(4, 128, 768)
    grad_gain_o[...] = jnp.sum(grad_normed * values * rms_scale(values), axis=0, keepdims=True)


def finish_kernel(x, parts, grad_after, gain, out):
    values = x[...].astype(F32)
    grad_normed = jnp.sum(parts[...].astype(F32), axis=0)
    out[...] = (
        grad_after[...] + rms_back(grad_normed, values, rms_scale(values), gain[...])
    ).astype(BF)


def sum_kernel(a, b, a_o, b_o):
    a_o[...] = jnp.sum(a[...].astype(F32), axis=0)
    b_o[...] = jnp.sum(b[...].astype(F32), axis=0)


def choose_matrix():
    choose = np.zeros((2 * EXPERTS * CAP, EXPERTS * SLOT), np.float32)
    for kind in range(2):
        for source in range(EXPERTS):
            for slot in range(CAP):
                choose[
                    kind * EXPERTS * CAP + source * CAP + slot, source * SLOT + kind * CAP + slot
                ] = 1.0
    return choose


def shape(*dims, dtype=BF):
    return jax.ShapeDtypeStruct(dims, dtype)


def body(
    inputs,
    cotangent,
    routes,
    drop_mask,
    buckets,
    qkv_weight,
    out_weight,
    router_weight,
    attn_gain,
    ffn_gain,
    bias_table,
    expert_in,
    expert_out,
):
    f = flat_id()
    m, g = f % 4, f // 4
    plane = g // 8
    choose = jnp.asarray(choose_matrix(), BF)
    offsets = jnp.pad(buckets, (0, 1), constant_values=-1).reshape(1, 512)
    drop = drop_mask.reshape(128, 1)

    quarters = qkv_weight.reshape(6, 3, 4, 192).transpose(2, 0, 1, 3).reshape(4, 6, 576)
    small = jnp.concatenate(
        [
            router_weight,
            attn_gain[:, None],
            ffn_gain[:, None],
            jnp.pad(bias_table, (0, 3))[:, None],
            jnp.zeros((6, 45), BF),
        ],
        axis=1,
    )
    packed = jnp.concatenate([quarters, jnp.broadcast_to(small, (4, 6, 64))], axis=2)
    packed = jnp.pad(packed, ((0, 0), (0, 10), (0, 0)))
    tokens, packed, out_rows = exchange(
        0, QUAD, (inputs, True), (packed, False), (jnp.pad(out_weight, ((0, 10), (0, 0))), True)
    )
    wide, out_mine = gather_weights(
        1, packed[:, :6].reshape(24, 640), out_rows[:, :6].reshape(24, 768)
    )
    weights = wide.reshape(768, 640)
    out_mine = out_mine.reshape(192, 768)
    router = weights[:, 576:592]
    gains = weights[:, 592:594].astype(F32).T
    gain_one, gain_two = gains[0:1], gains[1:2]
    table = wide[:, :, 594].reshape(BUCKETS, 4, 6)[:, :, :3]
    table = lax.dynamic_index_in_dim(table, m, 1, keepdims=False).T
    table = jnp.pad(table, ((0, 5), (0, 0)))

    normed, proj, probs, mixed, parts = compute(
        attend_kernel,
        [
            shape(512, 768),
            shape(512, 576),
            shape(6, 256, 256, dtype=F32),
            shape(512, 192),
            shape(4, 128, 768),
        ],
        tokens,
        weights,
        out_mine,
        gain_one,
        table,
        offsets,
    )
    (parts,) = exchange(2, QUAD, (parts, False))
    after, normed_two, router_probs, pick, send = compute(
        route_kernel,
        [
            shape(128, 768, dtype=F32),
            shape(128, 768),
            shape(128, EXPERTS, dtype=F32),
            shape(256, EXPERTS * SLOT),
            shape(EXPERTS, SLOT, 768),
        ],
        inputs,
        parts,
        gain_two,
        router,
        routes,
        drop,
        cotangent,
    )
    (arrived,) = exchange(3, SAME_R, (send, False))
    rows = compute(compact_kernel, shape(320, 768), choose, arrived)
    (rows,) = exchange(4, PLANE, (rows, True))
    (rows,) = exchange(5, MATE, (rows, True))
    parts, grad_expert_in, grad_expert_out = experts(
        rows.reshape(8, 2, 160, 768), expert_in, expert_out
    )
    (parts,) = exchange(6, MATE, (parts.reshape(2, 4, 320, 768), False))
    parts = compute(add_kernel, shape(4, 320, 768), parts)
    (parts,) = exchange(7, PLANE, (parts, False))
    back = compute(expand_kernel, shape(EXPERTS, SLOT, 768), choose, parts)
    (back,) = exchange(8, SAME_R, (back, False))
    result, grad_after, grad_low, grad_router, grad_gain_two = compute(
        after_kernel,
        [
            shape(128, 768),
            shape(128, 768, dtype=F32),
            shape(128, 768),
            shape(768, EXPERTS, dtype=F32),
            shape(1, 768, dtype=F32),
        ],
        back,
        pick,
        after,
        normed_two,
        router_probs,
        routes,
        drop,
        cotangent,
        gain_two,
        router,
    )
    (grad_proj,) = exchange(9, QUAD, (grad_low, True))
    grad_qkv, grad_out, parts, grad_gain_one, grad_table = compute(
        attend_back_kernel,
        [
            shape(768, 576, dtype=F32),
            shape(8, 24, 768),
            shape(4, 128, 768),
            shape(1, 768, dtype=F32),
            shape(8, BUCKETS, dtype=F32),
        ],
        tokens,
        normed,
        proj,
        probs,
        mixed,
        grad_proj,
        weights,
        out_mine,
        offsets,
    )
    grad_bias = lax.dynamic_update_slice(
        jnp.zeros((BUCKETS, 4, 6), F32), grad_table[:3].T.reshape(BUCKETS, 1, 3), (0, m, 0)
    )
    grad_wide = jnp.concatenate(
        [
            grad_qkv,
            grad_router,
            grad_gain_one.T,
            grad_gain_two.T,
            grad_bias.reshape(768, 1),
            jnp.zeros((768, 45), F32),
        ],
        axis=1,
    ).astype(BF)
    (parts,) = exchange(10, QUAD, (parts, False))
    grad_input = compute(
        finish_kernel, shape(128, 768), inputs, parts, grad_after, gain_one
    )
    got_wide, got_out = scatter_grads(11, grad_wide.reshape(32, 24, 640), grad_out)
    sum_wide, sum_out = compute(
        sum_kernel, [shape(24, 640, dtype=F32), shape(24, 768, dtype=F32)], got_wide, got_out
    )
    final = jnp.concatenate([sum_wide, sum_out], axis=1).reshape(4, 6, 1408)
    (final,) = exchange(12, QUAD, (jnp.pad(final, ((0, 0), (0, 2), (0, 0))), False))
    final = final[:, :6]
    small = jnp.sum(final[:, :, 576:640], axis=0)
    grad_qkv = final[:, :, :576].reshape(4, 6, 3, 192).transpose(1, 2, 0, 3).reshape(6, 2304)
    grad_out = lax.dynamic_index_in_dim(final[:, :, 640:], plane, 0, keepdims=False)
    return (
        result,
        grad_input,
        grad_qkv,
        grad_out,
        small[:, :16],
        small[:, 16],
        small[:, 17],
        small[:3, 18],
        grad_expert_in,
        grad_expert_out,
    )


def solution(mesh):
    placed = (
        P(("fsdp", "sp"), None),
        P(("fsdp", "sp"), None),
        P(("fsdp", "sp"), None),
        P(("fsdp", "sp")),
        P(),
        P(("fsdp", "sp"), None),
        P(("fsdp", "sp"), None),
        P(("fsdp", "sp"), None),
        P(("fsdp", "sp")),
        P(("fsdp", "sp")),
        P(("fsdp", "sp")),
        P(None, ("fsdp", "sp")),
        P(("fsdp", "sp"), None),
    )
    return jax.shard_map(
        body,
        mesh=mesh,
        in_specs=placed,
        out_specs=(
            P(("fsdp", "sp"), None),
            P(("fsdp", "sp"), None),
            P(("fsdp", "sp"), None),
            P(("fsdp", "sp"), None),
            P(("fsdp", "sp"), None),
            P(("fsdp", "sp")),
            P(("fsdp", "sp")),
            P(("fsdp", "sp")),
            P(None, ("fsdp", "sp")),
            P(("fsdp", "sp"), None),
        ),
        check_vma=False,
    )
```

time: 1830 us -> 406 us (0.22)
  blocking collectives: 803 us -> 0 us
  local copies, waits for them, and re-layouts: 543 us -> 57.1 us
  Pallas kernels: 0 us -> 342 us
  starting transfers between devices: 217 us -> 0 us
  waiting for transfers between devices: 168 us -> 0 us
  matrix products: 50.7 us -> 0 us
    unnamed x3 -> x0, blocking collectives: 493 us -> none
    gather x3 -> x0, local copies, waits for them, and re-layouts: 412 us -> none  [the longest x1 408 us: bucket_block(): picked = jnp.take(buckets, relative, axis=0).reshape(block_rows, length)]
    pallas_call x0 -> x23, Pallas kernels: none -> 342 us  [the longest x11 262 us: exchange(): pl.pallas_call(functools.partial(exchange_kernel, group, kinds), out_shap...]
    all_gather x1 -> x0, blocking collectives: 310 us -> none  [body(): lax.all_gather(router_weight, ('fsdp', 'sp'), axis=0, tiled=True)]
    unnamed x64 -> x0, starting transfers between devices: 177 us -> none
    all_to_all x8 -> x0, waiting for transfers between devices: 166 us -> none  [the longest x1 41.9 us: body(): lax.all_to_all(grad_slots, ('fsdp', 'sp'), split_axis=0, concat_axis=0, t...]
    dot_general x25 -> x0, matrix products: 50.7 us -> none  [the longest x1 5.65 us: body(): pre_rows = jnp.dot(flat_rows, expert_in, preferred_element_type=jnp.float32)]
    unnamed x242 -> x102, local copies, waits for them, and re-layouts: 79.3 us -> 38.1 us
  transfers between devices with their start and end apart: 74 -> 0, of which waited for: 8 -> 0; matrix products, arithmetic and copies ran while one was open for 28% -> 0% of each run, Pallas kernels for 0% -> 0%
where the time goes in v1:
time: 406 us; the launch traced here: 404 us
  Pallas kernels  342 us (84%)
  local copies, waits for them, and re-layouts  57.1 us (14%)
  other arithmetic  4.33 us (1%)
    pallas_call x11, Pallas kernels, exchange(): pl.pallas_call(functools.partial(exchange_kernel, group, kinds), out_shap...  262 us
    unnamed x102, local copies, waits for them, and re-layouts  38.1 us
    pallas_call x1, Pallas kernels, gather_weights(): pl.pallas_call(weights_kernel, out_shape=[jax.ShapeDtypeStruct((32,) + a....  28.9 us
    pallas_call x1, Pallas kernels, scatter_grads(): pl.pallas_call(grads_kernel, out_shape=[jax.ShapeDtypeStruct(a.shape, a.d...  23.9 us
    pallas_call x9, Pallas kernels, compute(): pl.pallas_call(kernel, out_shape=out, compiler_params=pltpu.CompilerParam...  15.3 us
    pallas_call x1, Pallas kernels, experts(): pl.pallas_call(expert_kernel, grid=(4,), out_shape=[jax.ShapeDtypeStruct(...  11.2 us

profile of v1, /device:TPU:1, one launch (start us, length us, event | category | flops | bytes accessed | tf_op | source)
XLA Modules:
  0.0 404.4 jit_solution(16486914792251550400)
XLA Ops:
  5.5 1.3 pad.26.refs_2_
  6.8 14.5 %shard_map.213 = (bf16[4,128,768]{2,1,0:T(8,128)(2,1)}, bf16[4,16,640]{2,1,0:T(8,128)(2,1)}, bf16[4,16,768]{2,1,0:T(8,128)(2,1)}) custom-call(bf16[128,768]{1,0:T(8,128)(2,1)} %x.15, bf16[4,16,640]{2,1,0:T(8,128)(2,1)} %fusion.2.refs_1_, bf16[16,768]{1,0:T(8,128)(2,1)} %pad.26.refs_2_), custom_call_target="tpu_custom_call" | custom-call | bytes 1933312 | tf_op jit(solution)/shard_map/pallas_call | solution.py:132
  24.2 28.9 %shard_map.214 = (bf16[32,24,640]{2,1,0:T(8,128)(2,1)}, bf16[8,24,768]{2,1,0:T(8,128)(2,1)}) custom-call(bf16[24,640]{1,0:T(8,128)(2,1)} %reshape.80.a_in, bf16[24,768]{1,0:T(8,128)(2,1)} %reshape.81.b_in), custom_call_target="tpu_custom_call" | custom-call | tf_op jit(solution)/shard_map/pallas_call | solution.py:200
  56.8 2.9 shard_map.215
  63.3 11.3 %shard_map.216.parts = bf16[4,128,768]{2,1,0:T(8,128)(2,1)} custom-call(bf16[4,128,768]{2,1,0:T(8,128)(2,1)} %copy-done.22), custom_call_target="tpu_custom_call" | custom-call | bytes 1572864 | tf_op jit(solution)/shard_map/pallas_call | solution.py:132
  82.3 15.7 %shard_map.218.x = bf16[16,24,768]{2,1,0:T(8,128)(2,1)} custom-call(bf16[16,24,768]{2,1,0:T(8,128)(2,1)} %copy-done.27), custom_call_target="tpu_custom_call" | custom-call | bytes 1179648 | tf_op jit(solution)/shard_map/pallas_call | solution.py:132
  100.3 23.7 %shard_map.220.refs_0_ = bf16[4,320,768]{2,1,0:T(8,128)(2,1)} custom-call(bf16[320,768]{1,0:T(8,128)(2,1)} %copy-done.12), custom_call_target="tpu_custom_call" | custom-call | bytes 3932160 | tf_op jit(solution)/shard_map/pallas_call | solution.py:132
  124.0 62.4 %shard_map.221 = bf16[2,4,320,768]{3,2,1,0:T(8,128)(2,1)} custom-call(bf16[4,320,768]{2,1,0:T(8,128)(2,1)} %shard_map.220.refs_0_), custom_call_target="tpu_custom_call" | custom-call | bytes 7864320 | tf_op jit(solution)/shard_map/pallas_call | solution.py:132
  188.6 11.2 %shard_map.222 = (bf16[8,2,160,768]{3,2,1,0:T(8,128)(2,1)S(1)}, f32[768,384]{1,0:T(8,128)}, f32[384,768]{1,0:T(8,128)}) custom-call(bf16[8,2,160,768]{3,2,1,0:T(8,128)(2,1)} %bitcast.45, bf16[768,384]{1,0:T(8,128)(2,1)S(1)} %copy-done.44, bf16[384,768]{1,0:T(8,128)(2,1)S(1)} %copy-done.45), custom_call_target="tpu_custom_call" | custom-call | flops 4529848320 | bytes 12000000 | tf_op jit(solution)/shard_map/pallas_call | solution.py:433
  199.8 1.9 copy-done.4
  201.6 60.7 %shard_map.223.x = bf16[2,4,320,768]{3,2,1,0:T(8,128)(2,1)} custom-call(bf16[2,4,320,768]{3,2,1,0:T(8,128)(2,1)} %bitcast.40), custom_call_target="tpu_custom_call" | custom-call | bytes 7864320 | tf_op jit(solution)/shard_map/pallas_call | solution.py:132
  262.4 2.1 copy-done
  264.9 1.3 copy-done.2
  266.2 23.4 %shard_map.225.x = bf16[4,320,768]{2,1,0:T(8,128)(2,1)} custom-call(bf16[4,320,768]{2,1,0:T(8,128)(2,1)} %copy-done.2), custom_call_target="tpu_custom_call" | custom-call | bytes 3932160 | tf_op jit(solution)/shard_map/pallas_call | solution.py:132
  289.7 1.5 copy-done.1
  292.6 14.5 %shard_map.227.back = bf16[16,24,768]{2,1,0:T(8,128)(2,1)} custom-call(bf16[16,24,768]{2,1,0:T(8,128)(2,1)} %copy-done.10), custom_call_target="tpu_custom_call" | custom-call | bytes 1179648 | tf_op jit(solution)/shard_map/pallas_call | solution.py:132
  312.7 1.6 shard_map.228
  316.5 13.1 %shard_map.229.grad_proj = bf16[4,128,768]{2,1,0:T(8,128)(2,1)} custom-call(bf16[128,768]{1,0:T(8,128)(2,1)} %copy-done.41), custom_call_target="tpu_custom_call" | custom-call | bytes 1572864 | tf_op jit(solution)/shard_map/pallas_call | solution.py:132
  332.8 7.1 %shard_map.230 = (f32[768,576]{1,0:T(8,128)}, bf16[8,24,768]{2,1,0:T(8,128)(2,1)S(1)}, bf16[4,128,768]{2,1,0:T(8,128)(2,1)S(1)}, f32[1,768]{1,0:T(1,128)S(1)}, f32[8,32]{1,0:T(8,128)S(1)}) custom-call(bf16[4,128,768]{2,1,0:T(8,128)(2,1)S(1)} %copy-done.7, bf16[512,768]{1,0:T(8,128)(2,1)S(1)} %get-tuple-element.55.normed, bf16[512,576]{1,0:T(8,128)(2,1)S(1)} %copy-done.24, ...), custom_call_target="tpu_custom_call" | custom-call | bytes 5998592 | tf_op jit(solution)/shard_map/pallas_call | solution.py:304
  341.4 1.7 convert.23
  344.4 1.9 concatenate.31.a_in
  346.3 23.9 %shard_map.233 = (bf16[32,24,640]{2,1,0:T(8,128)(2,1)}, bf16[32,24,768]{2,1,0:T(8,128)(2,1)}) custom-call(bf16[32,24,640]{2,1,0:T(8,128)(2,1)} %concatenate.31.a_in, bf16[8,24,768]{2,1,0:T(8,128)(2,1)} %copy-done.34), custom_call_target="tpu_custom_call" | custom-call | tf_op jit(solution)/shard_map/pallas_call | solution.py:284
  373.7 11.2 %shard_map.235 = f32[4,8,1408]{2,1,0:T(8,128)} custom-call(f32[4,8,1408]{2,1,0:T(8,128)} %pad.29.refs_0_), custom_call_target="tpu_custom_call" | custom-call | bytes 360448 | tf_op jit(solution)/shard_map/pallas_call | solution.py:132
  390.5 11.8 %shard_map.231.parts = bf16[4,128,768]{2,1,0:T(8,128)(2,1)} custom-call(bf16[4,128,768]{2,1,0:T(8,128)(2,1)} %copy-done.21), custom_call_target="tpu_custom_call" | custom-call | bytes 1572864 | tf_op jit(solution)/shard_map/pallas_call | solution.py:132
  (155 shorter events, 53.5 us)
Async XLA Ops:
  0.6 55.1 %copy-start.47 = (s32[511]{0:T(512)S(1)}, s32[511]{0:T(512)}, u32[]{:S(2)}) copy-start(s32[511]{0:T(512)} %param.18) | copy-start | bytes 6136
  21.3 34.5 %copy-start.7 = (bf16[4,128,768]{2,1,0:T(8,128)(2,1)S(1)}, bf16[4,128,768]{2,1,0:T(8,128)(2,1)}, u32[]{:S(2)}) copy-start(bf16[4,128,768]{2,1,0:T(8,128)(2,1)} %get-tuple-element.42.x) | copy-start | bytes 2359300
  53.1 2.7 copy-start.3
  56.8 18.0 %copy-start.48 = (s32[128,1]{0,1:T(1,128)S(1)}, s32[128,1]{0,1:T(1,128)}, u32[]{:S(2)}) copy-start(s32[128,1]{0,1:T(1,128)} %param.16) | copy-start | bytes 1540
  56.8 18.1 %copy-start.49 = (s32[128]{0:T(128)S(1)}, s32[128]{0:T(128)}, u32[]{:S(2)}) copy-start(s32[128]{0:T(128)} %param.17) | copy-start | bytes 1540
  56.8 18.8 %copy-start.13 = (bf16[128,768]{1,0:T(8,128)(2,1)S(1)}, bf16[128,768]{1,0:T(8,128)(2,1)}, u32[]{:S(2)}) copy-start(bf16[128,768]{1,0:T(8,128)(2,1)} %x.15) | copy-start | bytes 589828
  56.8 18.8 %copy-start.20 = (bf16[128,768]{1,0:T(8,128)(2,1)S(1)}, bf16[128,768]{1,0:T(8,128)(2,1)}, u32[]{:S(2)}) copy-start(bf16[128,768]{1,0:T(8,128)(2,1)} %cot.3) | copy-start | bytes 589828
  59.7 1.2 copy-start.14
  74.6 23.4 %copy-start.19 = (bf16[320,384]{1,0:T(8,128)(2,1)S(1)}, bf16[320,384]{1,0:T(8,128)(2,1)}, u32[]{:S(2)}) copy-start(bf16[320,384]{1,0:T(8,128)(2,1)} %constant.66.clone.choose) | copy-start | bytes 737284
  75.6 1.1 copy-start.5
  186.5 1.1 copy-start.44
  199.8 1.9 copy-start.4
  262.4 2.1 copy-start
  264.9 1.3 copy-start.2
  289.7 1.5 copy-start.1
  292.6 36.9 %copy-start.16 = (bf16[8,24,768]{2,1,0:T(8,128)(2,1)S(1)}, bf16[8,24,768]{2,1,0:T(8,128)(2,1)}, u32[]{:S(2)}) copy-start(bf16[8,24,768]{2,1,0:T(8,128)(2,1)} %get-tuple-element.46) | copy-start | bytes 884740
  329.6 1.1 copy-start.8
  330.7 1.1 copy-start.24
  341.4 2.9 copy-start.29
  370.2 1.3 copy-start.17
  371.5 1.2 copy-start.18
  373.0 29.3 %copy-start.31 = (f32[128,768]{1,0:T(8,128)S(1)}, f32[128,768]{1,0:T(8,128)}, u32[]{:S(2)}) copy-start(f32[128,768]{1,0:T(8,128)} %copy-done.30) | copy-start | bytes 1179652
  389.1 15.4 %copy-start.46 = (f32[6,64]{1,0:T(8,128)}, f32[6,64]{1,0:T(8,128)S(1)}, u32[]{:S(2)}) copy-start(f32[6,64]{1,0:T(8,128)S(1)} %slice_reduce_fusion) | copy-start | bytes 4612
  402.4 1.1 copy-start.6
  (26 other events, 21.8 us)

commit v2 on v0

v2 whole, which is shorter than its diff:
```python
import functools

import jax
import jax.numpy as jnp
import numpy as np
from jax import lax
from jax.experimental import pallas as pl
from jax.experimental.pallas import tpu as pltpu
from jax.sharding import PartitionSpec as P

HEADS = 12
HEAD_DIM = 64
EXPERTS = 16
BUCKETS = 32
CAP = 10
EPSILON = 1e-06
MESH = pl.DeviceIdType.MESH
BF = jnp.bfloat16
F32 = jnp.float32
SLOT = 24
GELU_C = 0.7978845608028654
GELU_A = 0.044715
DEPTH = 2 * EXPERTS * CAP
HALF = EXPERTS * CAP


def coords(flat):
    return (lax.div(flat, 2), lax.rem(flat, 2))


def for_range(low, high, fn):
    def step(j, carry):
        fn(j)
        return carry

    lax.fori_loop(low, high, step, 0)


def dot(a, b, dims=((1,), (0,)), precision=None):
    return lax.dot_general(
        a, b, (dims, ((), ())), precision=precision, preferred_element_type=F32
    )


def rms_scale(values):
    return lax.rsqrt(jnp.mean(values * values, axis=-1, keepdims=True) + EPSILON)


def rms_back(grad, values, scale, gain):
    weighted = grad * gain
    inner = jnp.mean(weighted * values, axis=-1, keepdims=True)
    return scale * weighted - values * (scale * scale * scale * inner)


def iota(shape, dim):
    return lax.broadcasted_iota(jnp.int32, shape, dim)


def ones_where(mask):
    return mask.astype(F32).astype(BF)


class Links:
    def __init__(self, send, recv):
        self.send, self.recv, self.used = send, recv, 0

    def pair(self, count=1):
        first = self.used
        self.used += count
        return first

    def copy(self, index, source, target, device):
        return pltpu.make_async_remote_copy(
            src_ref=source,
            dst_ref=target,
            send_sem=self.send.at[index],
            recv_sem=self.recv.at[index],
            device_id=coords(device),
            device_id_type=MESH,
        )


def rows_of(ref):
    blocks, rows, width = ref.shape
    return ref[...].astype(F32).reshape(blocks * rows, width).astype(BF)


def layer_kernel(
    x,
    routes,
    drop,
    buckets,
    qkv,
    out_w,
    router_w,
    gain_attn,
    gain_ffn,
    bias_w,
    cot_any,
    expert_in_any,
    expert_out_any,
    choose_any,
    grad_input_o,
    grad_qkv_o,
    grad_out_o,
    grad_small_o,
    result_any,
    grad_in_any,
    grad_eout_any,
    cot,
    expert_in,
    expert_out,
    choose,
    result_s,
    grad_in_o,
    grad_eout_o,
    offsets,
    lines_s,
    packs,
    packs_in,
    rawb,
    rawb_in,
    lay_a,
    lay_b,
    chunk_a,
    chunk_b,
    wide,
    weights_s,
    outs,
    tokens,
    normed_s,
    proj_s,
    probs_s,
    mixed_s,
    part,
    from_mate,
    merge,
    to_x,
    from_x,
    after_s,
    normed_two_s,
    send_s,
    arrived,
    rows_s,
    parts_s,
    mate_parts,
    sums_s,
    got_x,
    got_z,
    diag_x,
    diag_z,
    back_s,
    back_in,
    grad_after_s,
    grad_low,
    grad_wide,
    grad_wide_in,
    grad_out_s,
    grad_out_in,
    fin,
    fin_in,
    send_sem,
    recv_sem,
    local_sem,
):
    loads = [
        pltpu.make_async_copy(source, target, local_sem.at[i])
        for i, (source, target) in enumerate(
            [
                (cot_any, cot),
                (expert_in_any, expert_in),
                (expert_out_any, expert_out),
                (choose_any, choose),
            ]
        )
    ]
    stores = [
        pltpu.make_async_copy(source, target, local_sem.at[4 + i])
        for i, (source, target) in enumerate(
            [(result_s, result_any), (grad_in_o, grad_in_any), (grad_eout_o, grad_eout_any)]
        )
    ]
    links = Links(send_sem, recv_sem)
    fs, sp = lax.axis_index("fsdp"), lax.axis_index("sp")
    f = fs * 2 + sp
    m, g = lax.rem(f, 4), lax.div(f, 4)
    plane, place = lax.div(g, 8), lax.rem(g, 8)
    core, x_lo = lax.div(m, 2), lax.rem(m, 2)
    expert, member = lax.div(f, 8), lax.rem(f, 8)
    z_lo = lax.div(member, 4)
    quad = f - m
    mate_m = (1 - core) * 2 + x_lo
    beside_m = core * 2 + (1 - x_lo)
    cross_m = (1 - core) * 2 + (1 - x_lo)
    mate, beside = quad + mate_m, quad + beside_m
    above = f - z_lo * 4 + (1 - z_lo) * 4
    spot = z_lo * 2 + x_lo
    spot_x = z_lo * 2 + (1 - x_lo)
    spot_z = (1 - z_lo) * 2 + x_lo
    spot_d = (1 - z_lo) * 2 + (1 - x_lo)

    barrier = pltpu.get_barrier_semaphore()

    def hello(device):
        pl.semaphore_signal(barrier, inc=1, device_id=coords(device), device_id_type=MESH)

    for j in range(1, 4):
        hello(quad + lax.rem(m + j, 4))
    for_range(1, 32, lambda j: hello(4 * lax.rem(g + j, 32) + m))

    for load in loads:
        load.start()
    tokens[m] = x[...]
    offsets[...] = jnp.full((1, 512), -1, jnp.int32)
    offsets[:, :511] = buckets[...]
    lines_s[...] = jnp.zeros((8, 128), F32)
    lines_s[0:1, 0:6] = gain_attn[...].astype(F32)
    lines_s[1:2, 0:6] = gain_ffn[...].astype(F32)
    lines_s[2:3, 0:3] = bias_w[...].astype(F32)
    lines_s[3:4] = routes[...].astype(F32)
    lines_s[4:5] = drop[...].astype(F32)
    columns_of = lines_s[...].T
    chosen = columns_of[:, 3:4].astype(jnp.int32)
    kept = columns_of[:, 4:5]
    weight = qkv[...].astype(F32)
    extra = jnp.concatenate(
        [router_w[...].astype(F32), columns_of[:6], jnp.zeros((6, 40), F32)], axis=1
    )
    for k in range(4):
        columns = [weight[:, 768 * i + 192 * k : 768 * i + 192 * k + 192] for i in range(3)]
        packs[k, 0:6] = jnp.concatenate(columns + [extra], axis=1).astype(BF)
    rawb[0:6] = out_w[...]
    pl.semaphore_wait(barrier, 34)

    base_p, base_b = links.pair(4), links.pair(4)

    def copy_pack(j):
        k = lax.rem(m + j, 4)
        return links.copy(base_p + j, packs.at[k], packs_in.at[m], quad + k)

    def copy_raw(j):
        return links.copy(base_b + j, rawb, rawb_in.at[m], quad + lax.rem(m + j, 4))

    for j in range(1, 4):
        copy_pack(j).start()
        copy_raw(j).start()
    packs_in[m] = packs[m]
    rawb_in[m] = rawb[...]

    def gather_four(buffer):
        first = links.pair(3)
        to_mate = links.copy(first, buffer.at[m], buffer.at[m], mate)
        to_beside = links.copy(first + 1, buffer.at[m], buffer.at[m], beside)
        passed = links.copy(first + 2, buffer.at[beside_m], buffer.at[beside_m], mate)
        return to_mate, to_beside, passed

    def finish_four(copies):
        to_mate, to_beside, passed = copies
        to_beside.wait_recv()
        passed.start()
        to_mate.wait()
        to_beside.wait_send()
        passed.wait()

    token_copies = gather_four(tokens)
    token_copies[1].start()
    token_copies[0].start()
    for j in range(1, 4):
        copy_pack(j).wait()
        copy_raw(j).wait()
    for k in range(4):
        lay_a[6 * k : 6 * k + 6] = packs_in[k].astype(F32)[0:6]
        lay_b[6 * k : 6 * k + 6] = rawb_in[k].astype(F32)[0:6]
    chunk_a[...] = lay_a[...].astype(BF)
    chunk_b[...] = lay_b[...].astype(BF)

    base_a = links.pair(32)
    base_o, base_r = links.pair(32), links.pair(8)

    def copy_a(j):
        return links.copy(base_a + j, chunk_a, wide.at[g], 4 * lax.rem(g + j, 32) + m)

    def copy_b(j, q):
        return pltpu.make_async_remote_copy(
            src_ref=chunk_b,
            dst_ref=outs.at[q],
            send_sem=send_sem.at[base_o + j],
            recv_sem=recv_sem.at[base_r + q],
            device_id=coords(4 * lax.rem(g + j, 32) + m),
            device_id_type=MESH,
        )

    for_range(1, 32, lambda j: copy_a(j).start())

    @pl.when(plane == m)
    def _():
        for_range(1, 32, lambda j: copy_b(j, place).start())
        outs[place] = chunk_b[...]

    wide[g] = chunk_a[...]
    finish_four(token_copies)
    values = tokens[...].astype(F32).reshape(512, 768)
    scaled = values * rms_scale(values)
    for_range(1, 32, lambda j: copy_a(j).wait())

    weights_s[...] = rows_of(wide)
    weights = weights_s[...]
    turned = weights[:, 512:640].astype(F32).T
    gain_one, gain_two, table = turned[80:81], turned[81:82], turned[82:83]
    router = weights[:, 576:592]
    bucket = offsets[...]
    head_row = (iota((32, 24, 128), 1).reshape(768, 128) == 6 * m + iota((768, 128), 1)).astype(F32)
    head_row = head_row.T[:8]
    head_row = jnp.where(iota((8, 768), 0) < 3, head_row, 0.0)
    in_bucket = iota((32, 24, 512), 0).reshape(768, 512) == bucket
    by_offset = dot((head_row * table).astype(BF), ones_where(in_bucket))
    normed = (scaled * gain_one).astype(BF)
    normed_s[...] = normed
    proj = dot(normed, weights[:, :576]).astype(BF)
    proj_s[...] = proj
    seqs = [[], []]
    for h in range(3):
        line = jnp.broadcast_to(by_offset[h : h + 1], (256, 512))
        bias = pltpu.roll(line, 257, 1, stride=1, stride_axis=0)[:, :256]
        for s in range(2):
            rows = slice(256 * s, 256 * s + 256)
            query = proj[rows, 64 * h : 64 * h + 64]
            key = proj[rows, 192 + 64 * h : 256 + 64 * h]
            value = proj[rows, 384 + 64 * h : 448 + 64 * h]
            scores = dot(query, key, ((1,), (1,))) + bias
            exponent = jnp.exp(scores - jnp.max(scores, axis=-1, keepdims=True))
            probs = exponent / jnp.sum(exponent, axis=-1, keepdims=True)
            probs_s[3 * s + h] = probs
            seqs[s].append(dot(probs.astype(BF), value).astype(BF))
    mixed = jnp.concatenate([jnp.concatenate(s, axis=1) for s in seqs], axis=0)
    mixed_s[...] = mixed

    def take_b(q):
        @pl.when(8 * m + q != g)
        def _():
            copy_b(1, q).wait_recv()

    for_range(0, 8, take_b)

    @pl.when(plane == m)
    def _():
        for_range(1, 32, lambda j: copy_b(j, place).wait_send())

    out_mine = rows_of(outs)
    part[0] = dot(mixed, out_mine).astype(BF).reshape(4, 128, 768)

    def reduce_start(n):
        first = links.pair(3)
        cross = links.copy(first, part.at[n, cross_m], merge.at[n], mate)
        straight = links.copy(first + 1, part.at[n, mate_m], from_mate.at[n], mate)
        over = links.copy(first + 2, to_x.at[n], from_x.at[n], beside)
        cross.start()
        straight.start()
        return cross, straight, over

    def reduce_pass(n, copies):
        cross, straight, over = copies
        cross.wait()
        to_x[n] = (part[n, beside_m].astype(F32) + merge[n].astype(F32)).astype(BF)
        over.start()

    def reduce_end(n, copies):
        cross, straight, over = copies
        straight.wait()
        over.wait()
        return part[n, m].astype(F32) + from_mate[n].astype(F32) + from_x[n].astype(F32)

    copies = reduce_start(0)
    reduce_pass(0, copies)
    hot = chosen == iota((128, EXPERTS), 1)
    earlier = iota((128, 128), 1) < iota((128, 128), 0)
    counts = dot(ones_where(earlier), ones_where(hot))
    slot = jnp.sum(jnp.where(hot, counts, 0.0), axis=-1, keepdims=True).astype(jnp.int32)
    target = jnp.where(kept > 0, chosen * SLOT + slot, -SLOT)
    lanes = iota((128, EXPERTS * SLOT), 1)
    pick_row, pick_grad = ones_where(lanes == target), ones_where(lanes == target + CAP)
    loads[0].wait()
    grad = cot[...].astype(F32)
    after = x[...].astype(F32) + reduce_end(0, copies)
    after_s[...] = after
    normed_two = (after * rms_scale(after) * gain_two).astype(BF)
    normed_two_s[...] = normed_two
    logits = dot(normed_two, router)
    exponent = jnp.exp(logits - jnp.max(logits, axis=-1, keepdims=True))
    router_probs = exponent / jnp.sum(exponent, axis=-1, keepdims=True)
    gates = jnp.sum(jnp.where(hot, router_probs, 0.0), axis=-1, keepdims=True)
    grad_y = (grad * (kept * gates)).astype(BF)
    slots = dot(
        jnp.concatenate([pick_row, pick_grad], axis=0),
        jnp.concatenate([normed_two, grad_y], axis=0),
        ((0,), (0,)),
    )
    send_s[...] = slots.astype(BF).reshape(EXPERTS, SLOT, 768)

    def spread(source, target, base):
        def copy(j):
            k = lax.rem(expert + j, EXPERTS)
            return links.copy(base + j, source.at[k], target.at[expert], 8 * k + member)

        return copy

    copy_d = spread(send_s, arrived, links.pair(EXPERTS))
    for_range(1, EXPERTS, lambda j: copy_d(j).start())
    arrived[expert] = send_s[expert]
    grad_in_o[...] = jnp.zeros_like(grad_in_o)
    grad_eout_o[...] = jnp.zeros_like(grad_eout_o)
    for_range(1, EXPERTS, lambda j: copy_d(j).wait())
    loads[3].wait()
    rows_s[spot, core] = dot(choose[...], rows_of(arrived)).astype(BF)
    first_half, second_half = pl.ds(0, HALF), pl.ds(HALF, HALF)

    def rows_copy(place_of, half, device):
        ref = rows_s.at[place_of, core, half]
        return links.copy(links.pair(), ref, ref, device)

    out_x2 = rows_copy(spot, second_half, beside)
    out_z1 = rows_copy(spot, first_half, above)
    out_x1 = rows_copy(spot, first_half, beside)
    out_z2 = rows_copy(spot, second_half, above)
    out_m1 = rows_copy(spot, first_half, mate)
    out_m2 = rows_copy(spot, second_half, mate)
    pass_x = rows_copy(spot_z, first_half, beside)
    pass_z = rows_copy(spot_x, second_half, above)
    mate_x1, mate_x2 = (rows_copy(spot_x, h, mate) for h in (first_half, second_half))
    mate_z1, mate_z2 = (rows_copy(spot_z, h, mate) for h in (first_half, second_half))
    mate_d1, mate_d2 = (rows_copy(spot_d, h, mate) for h in (first_half, second_half))
    for copy in (out_x2, out_z1, out_m1, out_m2, out_x1, out_z2):
        copy.start()

    def expert_step(place_of):
        def to_mate(half):
            copy = links.copy(
                links.pair(),
                parts_s.at[place_of, 1 - core, half],
                mate_parts.at[place_of, half],
                mate,
            )
            copy.start()
            return copy

        both = rows_s[place_of]
        row = both[:, :HALF].reshape(DEPTH, 768)
        grad_row = both[:, HALF:].reshape(DEPTH, 768)
        pre = dot(row, expert_in[...])
        square = pre * pre
        tanh = jnp.tanh(GELU_C * (pre + GELU_A * (pre * square)))
        half = 0.5 * (1.0 + tanh)
        act = (pre * half).astype(BF)
        slope = half + (0.5 * GELU_C) * pre * (1.0 - tanh * tanh) * (1.0 + 3.0 * GELU_A * square)
        parts_s[place_of, :, :HALF] = dot(act, expert_out[...]).astype(BF).reshape(2, HALF, 768)
        one = to_mate(first_half)
        grad_act = dot(grad_row, expert_out[...], ((1,), (1,)))
        grad_pre = (grad_act * slope).astype(BF)
        parts_s[place_of, :, HALF:] = (
            dot(grad_pre, expert_in[...], ((1,), (1,))).astype(BF).reshape(2, HALF, 768)
        )
        two = to_mate(second_half)
        grad_in_o[...] += dot(row, grad_pre, ((0,), (0,)))
        grad_eout_o[...] += dot(act, grad_row, ((0,), (0,)))
        one.wait()
        two.wait()
        sums_s[place_of] = (
            parts_s[place_of, core].astype(F32) + mate_parts[place_of].astype(F32)
        ).astype(BF)

    def sums_copy(place_of, half, target, device):
        copy = links.copy(links.pair(), sums_s.at[place_of, half], target, device)
        copy.start()
        return copy

    loads[1].wait()
    loads[2].wait()
    out_m1.wait()
    out_m2.wait()
    expert_step(spot)
    out_x2.wait()
    pass_z.start()
    mate_x2.start()
    out_z1.wait()
    pass_x.start()
    mate_z1.start()
    out_x1.wait()
    mate_x1.start()
    out_z2.wait()
    mate_z2.start()
    mate_x2.wait()
    mate_x1.wait()
    expert_step(spot_x)
    x_one = sums_copy(spot_x, first_half, got_x.at[first_half], beside)
    pass_z.wait()
    mate_d2.start()
    pass_x.wait()
    mate_d1.start()
    mate_z1.wait()
    mate_z2.wait()
    expert_step(spot_z)
    z_two = sums_copy(spot_z, second_half, got_z.at[second_half], above)
    mate_d1.wait()
    mate_d2.wait()
    expert_step(spot_d)
    d_one = sums_copy(spot_d, first_half, diag_x, beside)
    d_two = sums_copy(spot_d, second_half, diag_z, above)
    stores[1].start()
    stores[2].start()
    d_one.wait()
    sums_s[spot_z, :HALF] = (sums_s[spot_z, :HALF].astype(F32) + diag_x[...].astype(F32)).astype(
        BF
    )
    z_one = sums_copy(spot_z, first_half, got_z.at[first_half], above)
    d_two.wait()
    sums_s[spot_x, HALF:] = (sums_s[spot_x, HALF:].astype(F32) + diag_z[...].astype(F32)).astype(
        BF
    )
    x_two = sums_copy(spot_x, second_half, got_x.at[second_half], beside)
    for copy in (x_one, z_two, z_one, x_two):
        copy.wait()
    total = sums_s[spot].astype(F32) + got_x[...].astype(F32) + got_z[...].astype(F32)
    back_s[...] = (
        dot(choose[...], total.astype(BF), ((0,), (0,))).astype(BF).reshape(EXPERTS, SLOT, 768)
    )
    copy_r = spread(back_s, back_in, links.pair(EXPERTS))
    for_range(1, EXPERTS, lambda j: copy_r(j).start())
    back_in[expert] = back_s[expert]
    for_range(1, EXPERTS, lambda j: copy_r(j).wait())

    flat = rows_of(back_in)
    expert_y = dot(pick_row, flat)
    slot_grad = dot(pick_grad, flat)
    after = after_s[...]
    grad_gate = kept * jnp.sum(grad * expert_y, axis=-1, keepdims=True)
    grad_logits = ((grad_gate * gates) * (hot.astype(F32) - router_probs)).astype(BF)
    grad_normed = dot(grad_logits, router, ((1,), (1,))) + slot_grad
    scale = rms_scale(after)
    grad_after = grad + rms_back(grad_normed, after, scale, gain_two)
    grad_after_s[...] = grad_after
    grad_low[m] = grad_after.astype(BF)
    low_copies = gather_four(grad_low)
    low_copies[1].start()
    low_copies[0].start()
    result_s[...] = (after + (kept * gates) * expert_y).astype(BF)
    stores[0].start()
    grad_router = dot(grad_logits, normed_two_s[...], ((0,), (0,)))
    grad_gain_two = jnp.sum(grad_normed * after * scale, axis=0, keepdims=True)
    finish_four(low_copies)

    grad_proj = grad_low[...].reshape(512, 768)
    grad_mixed = dot(grad_proj, out_mine, ((1,), (1,))).astype(BF)
    grad_out = dot(mixed_s[...], grad_proj, ((0,), (0,)))
    grad_out_s[...] = grad_out.astype(BF).reshape(8, 24, 768)
    base_gs, base_gr = links.pair(8), links.pair(32)

    def copy_go(q):
        p = 8 * m + q
        return pltpu.make_async_remote_copy(
            src_ref=grad_out_s.at[q],
            dst_ref=grad_out_in.at[g],
            send_sem=send_sem.at[base_gs + q],
            recv_sem=recv_sem.at[base_gr + lax.rem(p - g + 32, 32)],
            device_id=coords(4 * p + m),
            device_id_type=MESH,
        )

    def away(q, fn):
        @pl.when(8 * m + q != g)
        def _():
            fn(q)

    for_range(0, 8, lambda q: away(q, lambda k: copy_go(k).start()))
    flip = ones_where(iota((256, 256), 0) + iota((256, 256), 1) == 255)
    pieces = [[[], [], []], [[], [], []]]
    sums = []
    for h in range(3):
        mirrored = jnp.zeros((256, 256), F32)
        for s in range(2):
            rows = slice(256 * s, 256 * s + 256)
            query = proj_s[rows, 64 * h : 64 * h + 64]
            key = proj_s[rows, 192 + 64 * h : 256 + 64 * h]
            value = proj_s[rows, 384 + 64 * h : 448 + 64 * h]
            grad_rows = grad_mixed[rows, 64 * h : 64 * h + 64]
            probs = probs_s[3 * s + h]
            grad_probs = dot(grad_rows, value, ((1,), (1,)))
            inner = jnp.sum(probs * grad_probs, axis=-1, keepdims=True)
            grad_scores = (probs * (grad_probs - inner)).astype(BF)
            mirrored = mirrored + dot(flip, grad_scores)
            pieces[s][0].append(dot(grad_scores, key).astype(BF))
            pieces[s][1].append(dot(grad_scores, query, ((0,), (0,))).astype(BF))
            pieces[s][2].append(dot(probs.astype(BF), grad_rows, ((0,), (0,))).astype(BF))
        line = jnp.concatenate([mirrored, jnp.zeros((256, 256), F32)], axis=1)
        line = pltpu.roll(line, 0, 1, stride=1, stride_axis=0)
        sums.append(jnp.sum(line, axis=0, keepdims=True))
    grad_heads = jnp.concatenate(
        [jnp.concatenate([p for part_of in s for p in part_of], axis=1) for s in pieces], axis=0
    )
    sums = jnp.concatenate(sums + [jnp.zeros((5, 512), F32)], axis=0)
    high = sums.astype(BF)
    rest = sums - high.astype(F32)
    middle = rest.astype(BF)
    low = (rest - middle.astype(F32)).astype(BF)
    in_bucket = iota((32, 24, 512), 0).reshape(768, 512) == offsets[...]
    grad_table = dot(
        jnp.concatenate([high.astype(F32), middle.astype(F32), low.astype(F32)], axis=0).astype(BF),
        ones_where(in_bucket),
        ((1,), (1,)),
    )
    grad_table = (grad_table[16:24] + grad_table[8:16]) + grad_table[0:8]
    grad_table = jnp.sum(grad_table * head_row, axis=0, keepdims=True)
    lines = jnp.concatenate(
        [
            grad_router,
            jnp.zeros((1, 768), F32),
            grad_gain_two,
            grad_table,
            jnp.zeros((45, 768), F32),
        ],
        axis=0,
    )
    grad_qkv = dot(normed_s[...], grad_heads, ((0,), (0,)))
    grad_wide[...] = (
        jnp.concatenate([grad_qkv, lines.T], axis=1).reshape(32, 24, 640).astype(BF)
    )
    base_w = links.pair(32)

    def copy_w(j):
        p = lax.rem(g + j, 32)
        return links.copy(base_w + j, grad_wide.at[p], grad_wide_in.at[g], 4 * p + m)

    for_range(1, 32, lambda j: copy_w(j).start())
    grad_normed = dot(grad_heads, weights_s[:, :576], ((1,), (1,)))
    part[1] = grad_normed.astype(BF).reshape(4, 128, 768)
    copies = reduce_start(1)
    grad_wide_in[g] = grad_wide[g]
    reduce_pass(1, copies)
    values = x[...].astype(F32)
    grad_input_o[...] = (
        grad_after_s[...] + rms_back(reduce_end(1, copies), values, rms_scale(values), gain_one)
    ).astype(BF)
    for_range(0, 8, lambda q: away(q, lambda k: copy_go(k).wait_send()))

    @pl.when(plane == m)
    def _():
        grad_out_in[g] = grad_out_s[place]

        def take(j):
            sender = lax.rem(g - j + 32, 32)
            pltpu.make_async_remote_copy(
                src_ref=grad_out_s.at[0],
                dst_ref=grad_out_in.at[sender],
                send_sem=send_sem.at[base_gs],
                recv_sem=recv_sem.at[base_gr + j],
                device_id=coords(4 * sender + m),
                device_id_type=MESH,
            ).wait_recv()

        for_range(1, 32, take)
        lay_b[...] = jnp.sum(grad_out_in[...].astype(F32), axis=0)

    for_range(1, 32, lambda j: copy_w(j).wait())
    lay_a[...] = jnp.sum(grad_wide_in[...].astype(F32), axis=0)

    for store in stores:
        store.wait()

    for k in range(4):
        fin[k, 0:6, 0:640] = lay_a[6 * k : 6 * k + 6]
        fin[k, 0:6, 640:1408] = lay_b[6 * k : 6 * k + 6]
    base_f = links.pair(4)

    def copy_f(j):
        k = lax.rem(m + j, 4)
        return links.copy(base_f + j, fin.at[k], fin_in.at[m], quad + k)

    for j in range(1, 4):
        copy_f(j).start()
    fin_in[m] = fin[m]
    for j in range(1, 4):
        copy_f(j).wait()
    grad_qkv = jnp.concatenate(
        [fin_in[k, 0:6, 192 * i : 192 * i + 192] for i in range(3) for k in range(4)], axis=1
    )
    grad_qkv_o[...] = grad_qkv
    by_row = jnp.sum(grad_qkv * qkv[...].astype(F32), axis=1, keepdims=True)
    by_row = by_row / columns_of[0:6, 0:1]
    grad_out_o[...] = fin_in[plane, 0:6, 640:1408]
    total = jnp.sum(fin_in[:, 0:6, 512:640], axis=0)
    total = jnp.where(iota((6, 128), 1) == 80, by_row, total)
    grad_small_o[...] = jnp.concatenate([total, jnp.zeros((2, 128), F32)], axis=0)


def results_kernel(
    result,
    grad_input,
    grad_qkv,
    grad_out,
    grad_small,
    grad_in,
    grad_eout,
    result_o,
    grad_input_o,
    grad_qkv_o,
    grad_out_o,
    grad_router_o,
    gain_one_o,
    gain_two_o,
    bias_o,
    grad_in_o,
    grad_eout_o,
    sems,
):
    whole = [
        (grad_in, grad_in_o),
        (grad_eout, grad_eout_o),
        (result, result_o),
        (grad_input, grad_input_o),
        (grad_qkv, grad_qkv_o),
        (grad_out, grad_out_o),
    ]
    copies = [
        pltpu.make_async_copy(source, target, sems.at[i])
        for i, (source, target) in enumerate(whole)
    ]
    for copy in copies:
        copy.start()
    values = grad_small[...]
    grad_router_o[...] = values[0:6, 64:80]
    lines = jnp.concatenate([values, jnp.zeros((120, 128), F32)], axis=0).T
    gain_one_o[...] = lines[80:81, 0:6]
    gain_two_o[...] = lines[81:82, 0:6]
    bias_o[...] = lines[82:83, 0:3]
    for copy in copies:
        copy.wait()


def choose_matrix():
    choose = np.zeros((DEPTH, EXPERTS * SLOT), np.float32)
    for kind in range(2):
        for source in range(EXPERTS):
            for slot in range(CAP):
                choose[
                    kind * HALF + source * CAP + slot, source * SLOT + kind * CAP + slot
                ] = 1.0
    return choose


def shape(*dims, dtype=BF):
    return jax.ShapeDtypeStruct(dims, dtype)


SCRATCH = [
    ((128, 768), BF),
    ((768, 384), BF),
    ((384, 768), BF),
    ((DEPTH, EXPERTS * SLOT), BF),
    ((128, 768), BF),
    ((768, 384), F32),
    ((384, 768), F32),
    ((1, 512), jnp.int32),
    ((8, 128), F32),
    ((4, 16, 640), BF),
    ((4, 16, 640), BF),
    ((16, 768), BF),
    ((4, 16, 768), BF),
    ((24, 640), F32),
    ((24, 768), F32),
    ((24, 640), BF),
    ((24, 768), BF),
    ((32, 24, 640), BF),
    ((768, 640), BF),
    ((8, 24, 768), BF),
    ((4, 128, 768), BF),
    ((512, 768), BF),
    ((512, 576), BF),
    ((6, 256, 256), F32),
    ((512, 192), BF),
    ((2, 4, 128, 768), BF),
    ((2, 128, 768), BF),
    ((2, 128, 768), BF),
    ((2, 128, 768), BF),
    ((2, 128, 768), BF),
    ((128, 768), F32),
    ((128, 768), BF),
    ((EXPERTS, SLOT, 768), BF),
    ((EXPERTS, SLOT, 768), BF),
    ((4, 2, DEPTH, 768), BF),
    ((4, 2, DEPTH, 768), BF),
    ((4, DEPTH, 768), BF),
    ((4, DEPTH, 768), BF),
    ((DEPTH, 768), BF),
    ((DEPTH, 768), BF),
    ((HALF, 768), BF),
    ((HALF, 768), BF),
    ((EXPERTS, SLOT, 768), BF),
    ((EXPERTS, SLOT, 768), BF),
    ((128, 768), F32),
    ((4, 128, 768), BF),
    ((32, 24, 640), BF),
    ((32, 24, 640), BF),
    ((8, 24, 768), BF),
    ((32, 24, 768), BF),
    ((4, 8, 1408), F32),
    ((4, 8, 1408), F32),
]
TRANSFERS = 256


def body(
    inputs,
    cotangent,
    routes,
    drop_mask,
    buckets,
    qkv_weight,
    out_weight,
    router_weight,
    attn_gain,
    ffn_gain,
    bias_table,
    expert_in,
    expert_out,
):
    vmem = pl.BlockSpec(memory_space=pltpu.VMEM)
    anywhere = pl.BlockSpec(memory_space=pl.ANY)
    outputs = pl.pallas_call(
        layer_kernel,
        out_shape=[
            shape(128, 768),
            shape(6, 2304, dtype=F32),
            shape(6, 768, dtype=F32),
            shape(8, 128, dtype=F32),
            shape(128, 768),
            shape(768, 384, dtype=F32),
            shape(384, 768, dtype=F32),
        ],
        in_specs=[vmem] * 10 + [anywhere] * 4,
        out_specs=[vmem] * 4 + [anywhere] * 3,
        scratch_shapes=[pltpu.VMEM(dims, dtype) for dims, dtype in SCRATCH]
        + [
            pltpu.SemaphoreType.DMA((TRANSFERS,)),
            pltpu.SemaphoreType.DMA((TRANSFERS,)),
            pltpu.SemaphoreType.DMA((7,)),
        ],
        compiler_params=pltpu.CompilerParams(
            collective_id=0, has_side_effects=True, vmem_limit_bytes=60 * 1024 * 1024
        ),
    )(
        inputs,
        routes.reshape(1, 128),
        drop_mask.reshape(1, 128),
        buckets.reshape(1, 511),
        qkv_weight,
        out_weight,
        router_weight,
        attn_gain.reshape(1, 6),
        ffn_gain.reshape(1, 6),
        bias_table.reshape(1, 3),
        cotangent,
        expert_in,
        expert_out,
        jnp.asarray(choose_matrix(), BF),
    )
    grad_input, grad_qkv, grad_out, grad_small, result, grad_in, grad_eout = outputs
    final = pl.pallas_call(
        results_kernel,
        out_shape=[
            shape(128, 768),
            shape(128, 768),
            shape(6, 2304, dtype=F32),
            shape(6, 768, dtype=F32),
            shape(6, 16, dtype=F32),
            shape(1, 6, dtype=F32),
            shape(1, 6, dtype=F32),
            shape(1, 3, dtype=F32),
            shape(768, 384, dtype=F32),
            shape(384, 768, dtype=F32),
        ],
        in_specs=[vmem] * 7,
        out_specs=[anywhere] * 4 + [vmem] * 4 + [anywhere] * 2,
        scratch_shapes=[pltpu.SemaphoreType.DMA((6,))],
        compiler_params=pltpu.CompilerParams(vmem_limit_bytes=60 * 1024 * 1024),
    )(result, grad_input, grad_qkv, grad_out, grad_small, grad_in, grad_eout)
    return (
        *final[:5],
        final[5].reshape(6),
        final[6].reshape(6),
        final[7].reshape(3),
        *final[8:],
    )


def solution(mesh):
    placed = (
        P(("fsdp", "sp"), None),
        P(("fsdp", "sp"), None),
        P(("fsdp", "sp"), None),
        P(("fsdp", "sp")),
        P(),
        P(("fsdp", "sp"), None),
        P(("fsdp", "sp"), None),
        P(("fsdp", "sp"), None),
        P(("fsdp", "sp")),
        P(("fsdp", "sp")),
        P(("fsdp", "sp")),
        P(None, ("fsdp", "sp")),
        P(("fsdp", "sp"), None),
    )
    return jax.shard_map(
        body,
        mesh=mesh,
        in_specs=placed,
        out_specs=(
            P(("fsdp", "sp"), None),
            P(("fsdp", "sp"), None),
            P(("fsdp", "sp"), None),
            P(("fsdp", "sp"), None),
            P(("fsdp", "sp"), None),
            P(("fsdp", "sp")),
            P(("fsdp", "sp")),
            P(("fsdp", "sp")),
            P(None, ("fsdp", "sp")),
            P(("fsdp", "sp"), None),
        ),
        check_vma=False,
    )
```

time: 1830 us -> 150 us (0.08)
  blocking collectives: 803 us -> 0 us
  local copies, waits for them, and re-layouts: 543 us -> 0 us
  starting transfers between devices: 217 us -> 0 us
  waiting for transfers between devices: 168 us -> 0 us
  Pallas kernels: 0 us -> 149 us
  matrix products: 50.7 us -> 0 us
  other arithmetic: 19 us -> 0 us
    unnamed x3 -> x0, blocking collectives: 493 us -> none
    gather x3 -> x0, local copies, waits for them, and re-layouts: 412 us -> none  [the longest x1 408 us: bucket_block(): picked = jnp.take(buckets, relative, axis=0).reshape(block_rows, length)]
    all_gather x1 -> x0, blocking collectives: 310 us -> none  [body(): lax.all_gather(router_weight, ('fsdp', 'sp'), axis=0, tiled=True)]
    unnamed x64 -> x0, starting transfers between devices: 177 us -> none
    all_to_all x8 -> x0, waiting for transfers between devices: 166 us -> none  [the longest x1 41.9 us: body(): lax.all_to_all(grad_slots, ('fsdp', 'sp'), split_axis=0, concat_axis=0, t...]
    pallas_call x0 -> x2, Pallas kernels: none -> 149 us  [the longest x1 145 us: body(): pl.pallas_call(layer_kernel, out_shape=[shape(128, 768), shape(6, 2304, d...]
    unnamed x242 -> x0, local copies, waits for them, and re-layouts: 79.3 us -> none
    dot_general x25 -> x0, matrix products: 50.7 us -> none  [the longest x1 5.65 us: body(): pre_rows = jnp.dot(flat_rows, expert_in, preferred_element_type=jnp.float32)]
  transfers between devices with their start and end apart: 74 -> 0, of which waited for: 8 -> 0; matrix products, arithmetic and copies ran while one was open for 28% -> 0% of each run, Pallas kernels for 0% -> 0%
where the time goes in v2:
time: 150 us
  Pallas kernels  149 us (99%)
    pallas_call x1, Pallas kernels, body(): pl.pallas_call(layer_kernel, out_shape=[shape(128, 768), shape(6, 2304, d...  145 us
    pallas_call x1, Pallas kernels, body(): pl.pallas_call(results_kernel, out_shape=[shape(128, 768), shape(128, 768...  4.04 us

profile of v2, /device:TPU:1, one launch (start us, length us, event | category | flops | bytes accessed | tf_op | source)
XLA Modules:
  0.0 150.3 jit_solution(12207228884268406787)
XLA Ops:
  0.6 145.4 %shard_map.213 = (bf16[128,768]{1,0:T(8,128)(2,1)}, f32[6,2304]{1,0:T(8,128)}, f32[6,768]{1,0:T(8,128)}, f32[8,128]{1,0:T(8,128)}, bf16[128,768]{1,0:T(8,128)(2,...) custom-call(bf16[128,768]{1,0:T(8,128)(2,1)} %x.1, s32[1,128]{1,0:T(1,128)} %bitcast.10, s32[1,128]{1,0:T(1,128)} %bitcast.11, ...), custom_call_target="tpu_custom_call" | custom-call | tf_op jit(solution)/shard_map/pallas_call | solution.py:827
  146.1 4.0 %shard_map.214 = (bf16[128,768]{1,0:T(8,128)(2,1)}, bf16[128,768]{1,0:T(8,128)(2,1)}, f32[6,2304]{1,0:T(8,128)}, f32[6,768]{1,0:T(8,128)}, f32[6,16]{1,0:T(8,128...) custom-call(bf16[128,768]{1,0:T(8,128)(2,1)} %get-tuple-element.27.result,, ...), custom_call_target="tpu_custom_call" | custom-call | tf_op jit(solution)/shard_map/pallas_call | solution.py:866

commit v3 on v2

--- a/solution.py
+++ b/solution.py
@@ -126,6 +126,7 @@
     chunk_b,
     wide,
     weights_s,
+    in_bucket,
     outs,
     tokens,
     normed_s,
@@ -188,6 +189,14 @@
     core, x_lo = lax.div(m, 2), lax.rem(m, 2)
     expert, member = lax.div(f, 8), lax.rem(f, 8)
     z_lo = lax.div(member, 4)
+    x_hi, own_place = lax.rem(lax.div(expert, 2), 2), lax.div(expert, 4) * 2 + lax.rem(expert, 2)
+
+    def side_of(k):
+        return lax.rem(lax.rem(lax.div(k, 2), 2) + x_hi, 2)
+
+    def place_in(k):
+        return lax.div(k, 4) * 2 + lax.rem(k, 2)
+
     quad = f - m
     mate_m = (1 - core) * 2 + x_lo
     beside_m = core * 2 + (1 - x_lo)
@@ -301,6 +310,9 @@
     finish_four(token_copies)
     values = tokens[...].astype(F32).reshape(512, 768)
     scaled = values * rms_scale(values)
+    head_row = (iota((32, 24, 128), 1).reshape(768, 128) == 6 * m + iota((768, 128), 1)).astype(F32)
+    head_row = jnp.where(iota((8, 768), 0) < 3, head_row.T[:8], 0.0)
+    in_bucket[...] = ones_where(iota((32, 24, 512), 0).reshape(768, 512) == offsets[...])
     for_range(1, 32, lambda j: copy_a(j).wait())
 
     weights_s[...] = rows_of(wide)
@@ -308,12 +320,7 @@
     turned = weights[:, 512:640].astype(F32).T
     gain_one, gain_two, table = turned[80:81], turned[81:82], turned[82:83]
     router = weights[:, 576:592]
-    bucket = offsets[...]
-    head_row = (iota((32, 24, 128), 1).reshape(768, 128) == 6 * m + iota((768, 128), 1)).astype(F32)
-    head_row = head_row.T[:8]
-    head_row = jnp.where(iota((8, 768), 0) < 3, head_row, 0.0)
-    in_bucket = iota((32, 24, 512), 0).reshape(768, 512) == bucket
-    by_offset = dot((head_row * table).astype(BF), ones_where(in_bucket))
+    by_offset = dot((head_row * table).astype(BF), in_bucket[...])
     normed = (scaled * gain_one).astype(BF)
     normed_s[...] = normed
     proj = dot(normed, weights[:, :576]).astype(BF)
@@ -329,7 +336,7 @@
             value = proj[rows, 384 + 64 * h : 448 + 64 * h]
             scores = dot(query, key, ((1,), (1,))) + bias
             exponent = jnp.exp(scores - jnp.max(scores, axis=-1, keepdims=True))
-            probs = exponent / jnp.sum(exponent, axis=-1, keepdims=True)
+            probs = exponent * (1.0 / jnp.sum(exponent, axis=-1, keepdims=True))
             probs_s[3 * s + h] = probs
             seqs[s].append(dot(probs.astype(BF), value).astype(BF))
     mixed = jnp.concatenate([jnp.concatenate(s, axis=1) for s in seqs], axis=0)
@@ -397,21 +404,55 @@
     )
     send_s[...] = slots.astype(BF).reshape(EXPERTS, SLOT, 768)
 
-    def spread(source, target, base):
-        def copy(j):
-            k = lax.rem(expert + j, EXPERTS)
-            return links.copy(base + j, source.at[k], target.at[expert], 8 * k + member)
-
-        return copy
-
-    copy_d = spread(send_s, arrived, links.pair(EXPERTS))
-    for_range(1, EXPERTS, lambda j: copy_d(j).start())
-    arrived[expert] = send_s[expert]
+    base_d, base_r = links.pair(EXPERTS), links.pair(EXPERTS)
+
+    def group_at(side, i):
+        return (lax.div(i, 2) * 2 + lax.rem(side + x_hi, 2)) * 2 + lax.rem(i, 2)
+
+    def pair_copy(base, k, source, target):
+        return pltpu.make_async_remote_copy(
+            src_ref=source,
+            dst_ref=target,
+            send_sem=send_sem.at[base + k],
+            recv_sem=recv_sem.at[base + expert],
+            device_id=coords(8 * k + member),
+            device_id_type=MESH,
+        )
+
+    def copy_d(k):
+        return pair_copy(base_d, k, send_s.at[k], arrived.at[side_of(k), own_place])
+
+    def arrival(side, i):
+        k = group_at(side, i)
+        return links.copy(base_d + k, send_s.at[k], arrived.at[side, i], 8 * k + member)
+
+    def copy_r(k):
+        return pair_copy(base_r, k, back_s.at[side_of(k), place_in(k)], back_in.at[expert])
+
+    def come_back(k):
+        return links.copy(base_r + k, back_s.at[0, 0], back_in.at[k], 8 * k + member)
+
+    def next_group(j):
+        return lax.rem(expert + j, EXPERTS)
+
+    for_range(1, EXPERTS, lambda j: copy_d(next_group(j)).start())
+    arrived[0, own_place] = send_s[expert]
     grad_in_o[...] = jnp.zeros_like(grad_in_o)
     grad_eout_o[...] = jnp.zeros_like(grad_eout_o)
-    for_range(1, EXPERTS, lambda j: copy_d(j).wait())
     loads[3].wait()
-    rows_s[spot, core] = dot(choose[...], rows_of(arrived)).astype(BF)
+
+    def take_rows(side):
+        def take(i):
+            if side == 0:
+                pl.when(i != own_place)(lambda: arrival(side, i).wait_recv())
+            else:
+                arrival(side, i).wait_recv()
+
+        for_range(0, 8, take)
+        rows_s[spot, core, HALF * side : HALF * side + HALF] = dot(
+            choose[...], rows_of(arrived.at[side])
+        ).astype(BF)
+
     first_half, second_half = pl.ds(0, HALF), pl.ds(HALF, HALF)
 
     def rows_copy(place_of, half, device):
@@ -429,41 +470,39 @@
     mate_x1, mate_x2 = (rows_copy(spot_x, h, mate) for h in (first_half, second_half))
     mate_z1, mate_z2 = (rows_copy(spot_z, h, mate) for h in (first_half, second_half))
     mate_d1, mate_d2 = (rows_copy(spot_d, h, mate) for h in (first_half, second_half))
-    for copy in (out_x2, out_z1, out_m1, out_m2, out_x1, out_z2):
+    take_rows(0)
+    for copy in (out_z1, out_x1, out_m1):
         copy.start()
+    take_rows(1)
+    for copy in (out_x2, out_z2, out_m2):
+        copy.start()
+    for_range(1, EXPERTS, lambda j: copy_d(next_group(j)).wait_send())
 
     def expert_step(place_of):
-        def to_mate(half):
-            copy = links.copy(
-                links.pair(),
-                parts_s.at[place_of, 1 - core, half],
-                mate_parts.at[place_of, half],
-                mate,
-            )
-            copy.start()
-            return copy
-
         both = rows_s[place_of]
-        row = both[:, :HALF].reshape(DEPTH, 768)
-        grad_row = both[:, HALF:].reshape(DEPTH, 768)
+        row = jnp.concatenate([both[:, :80], both[:, 160:240]], axis=1).reshape(DEPTH, 768)
+        grad_row = jnp.concatenate([both[:, 80:160], both[:, 240:]], axis=1).reshape(DEPTH, 768)
         pre = dot(row, expert_in[...])
         square = pre * pre
         tanh = jnp.tanh(GELU_C * (pre + GELU_A * (pre * square)))
         half = 0.5 * (1.0 + tanh)
         act = (pre * half).astype(BF)
         slope = half + (0.5 * GELU_C) * pre * (1.0 - tanh * tanh) * (1.0 + 3.0 * GELU_A * square)
-        parts_s[place_of, :, :HALF] = dot(act, expert_out[...]).astype(BF).reshape(2, HALF, 768)
-        one = to_mate(first_half)
+        out = dot(act, expert_out[...]).astype(BF).reshape(2, HALF, 768)
+        parts_s[place_of, :, :80] = out[:, :80]
+        parts_s[place_of, :, 160:240] = out[:, 80:]
         grad_act = dot(grad_row, expert_out[...], ((1,), (1,)))
         grad_pre = (grad_act * slope).astype(BF)
-        parts_s[place_of, :, HALF:] = (
-            dot(grad_pre, expert_in[...], ((1,), (1,))).astype(BF).reshape(2, HALF, 768)
+        out = dot(grad_pre, expert_in[...], ((1,), (1,))).astype(BF).reshape(2, HALF, 768)
+        parts_s[place_of, :, 80:160] = out[:, :80]
+        parts_s[place_of, :, 240:] = out[:, 80:]
+        swap = links.copy(
+            links.pair(), parts_s.at[place_of, 1 - core], mate_parts.at[place_of], mate
         )
-        two = to_mate(second_half)
+        swap.start()
         grad_in_o[...] += dot(row, grad_pre, ((0,), (0,)))
         grad_eout_o[...] += dot(act, grad_row, ((0,), (0,)))
-        one.wait()
-        two.wait()
+        swap.wait()
         sums_s[place_of] = (
             parts_s[place_of, core].astype(F32) + mate_parts[place_of].astype(F32)
         ).astype(BF)
@@ -478,14 +517,14 @@
     out_m1.wait()
     out_m2.wait()
     expert_step(spot)
-    out_x2.wait()
-    pass_z.start()
-    mate_x2.start()
     out_z1.wait()
     pass_x.start()
     mate_z1.start()
     out_x1.wait()
     mate_x1.start()
+    out_x2.wait()
+    pass_z.start()
+    mate_x2.start()
     out_z2.wait()
     mate_z2.start()
     mate_x2.wait()
@@ -520,13 +559,14 @@
     for copy in (x_one, z_two, z_one, x_two):
         copy.wait()
     total = sums_s[spot].astype(F32) + got_x[...].astype(F32) + got_z[...].astype(F32)
-    back_s[...] = (
-        dot(choose[...], total.astype(BF), ((0,), (0,))).astype(BF).reshape(EXPERTS, SLOT, 768)
-    )
-    copy_r = spread(back_s, back_in, links.pair(EXPERTS))
-    for_range(1, EXPERTS, lambda j: copy_r(j).start())
-    back_in[expert] = back_s[expert]
-    for_range(1, EXPERTS, lambda j: copy_r(j).wait())
+    total = total.astype(BF)
+    for side in range(2):
+        slots = dot(choose[...], total[HALF * side : HALF * side + HALF], ((0,), (0,)))
+        back_s[side] = slots.astype(BF).reshape(8, SLOT, 768)
+    for_range(1, EXPERTS, lambda j: copy_r(next_group(j)).start())
+    back_in[expert] = back_s[0, own_place]
+    for_range(1, EXPERTS, lambda j: come_back(next_group(j)).wait_recv())
+    for_range(1, EXPERTS, lambda j: copy_r(next_group(j)).wait_send())
 
     flat = rows_of(back_in)
     expert_y = dot(pick_row, flat)
@@ -601,10 +641,9 @@
     rest = sums - high.astype(F32)
     middle = rest.astype(BF)
     low = (rest - middle.astype(F32)).astype(BF)
-    in_bucket = iota((32, 24, 512), 0).reshape(768, 512) == offsets[...]
     grad_table = dot(
         jnp.concatenate([high.astype(F32), middle.astype(F32), low.astype(F32)], axis=0).astype(BF),
-        ones_where(in_bucket),
+        in_bucket[...],
         ((1,), (1,)),
     )
     grad_table = (grad_table[16:24] + grad_table[8:16]) + grad_table[0:8]
@@ -736,13 +775,11 @@
 
 
 def choose_matrix():
-    choose = np.zeros((DEPTH, EXPERTS * SLOT), np.float32)
+    choose = np.zeros((HALF, 8 * SLOT), np.float32)
     for kind in range(2):
-        for source in range(EXPERTS):
+        for source in range(8):
             for slot in range(CAP):
-                choose[
-                    kind * HALF + source * CAP + slot, source * SLOT + kind * CAP + slot
-                ] = 1.0
+                choose[kind * 80 + source * CAP + slot, source * SLOT + kind * CAP + slot] = 1.0
     return choose
 
 
@@ -754,7 +791,7 @@
     ((128, 768), BF),
     ((768, 384), BF),
     ((384, 768), BF),
-    ((DEPTH, EXPERTS * SLOT), BF),
+    ((HALF, 8 * SLOT), BF),
     ((128, 768), BF),
     ((768, 384), F32),
     ((384, 768), F32),
@@ -770,6 +807,7 @@
     ((24, 768), BF),
     ((32, 24, 640), BF),
     ((768, 640), BF),
+    ((768, 512), BF),
     ((8, 24, 768), BF),
     ((4, 128, 768), BF),
     ((512, 768), BF),
@@ -784,7 +822,7 @@
     ((128, 768), F32),
     ((128, 768), BF),
     ((EXPERTS, SLOT, 768), BF),
-    ((EXPERTS, SLOT, 768), BF),
+    ((2, 8, SLOT, 768), BF),
     ((4, 2, DEPTH, 768), BF),
     ((4, 2, DEPTH, 768), BF),
     ((4, DEPTH, 768), BF),
@@ -793,7 +831,7 @@
     ((DEPTH, 768), BF),
     ((HALF, 768), BF),
     ((HALF, 768), BF),
-    ((EXPERTS, SLOT, 768), BF),
+    ((2, 8, SLOT, 768), BF),
     ((EXPERTS, SLOT, 768), BF),
     ((128, 768), F32),
     ((4, 128, 768), BF),

time: 150 us -> 150 us (level)
  no operation moved by 1% of the time
where the time goes in v3:
time: 150 us
  Pallas kernels  149 us (99%)
    pallas_call x1, Pallas kernels, body(): pl.pallas_call(layer_kernel, out_shape=[shape(128, 768), shape(6, 2304, d...  145 us
    pallas_call x1, Pallas kernels, body(): pl.pallas_call(results_kernel, out_shape=[shape(128, 768), shape(128, 768...  4.04 us

profile of v3, /device:TPU:1, one launch (start us, length us, event | category | flops | bytes accessed | tf_op | source)
XLA Modules:
  0.0 150.1 jit_solution(14773946350824790433)
XLA Ops:
  0.6 145.2 %shard_map.213 = (bf16[128,768]{1,0:T(8,128)(2,1)}, f32[6,2304]{1,0:T(8,128)}, f32[6,768]{1,0:T(8,128)}, f32[8,128]{1,0:T(8,128)}, bf16[128,768]{1,0:T(8,128)(2,...) custom-call(bf16[128,768]{1,0:T(8,128)(2,1)} %x.1, s32[1,128]{1,0:T(1,128)} %bitcast.10, s32[1,128]{1,0:T(1,128)} %bitcast.11, ...), custom_call_target="tpu_custom_call" | custom-call | tf_op jit(solution)/shard_map/pallas_call | solution.py:865
  145.8 4.0 %shard_map.214 = (bf16[128,768]{1,0:T(8,128)(2,1)}, bf16[128,768]{1,0:T(8,128)(2,1)}, f32[6,2304]{1,0:T(8,128)}, f32[6,768]{1,0:T(8,128)}, f32[6,16]{1,0:T(8,128...) custom-call(bf16[128,768]{1,0:T(8,128)(2,1)} %get-tuple-element.27.result,, ...), custom_call_target="tpu_custom_call" | custom-call | tf_op jit(solution)/shard_map/pallas_call | solution.py:904

commit v4 on v3

--- a/solution.py
+++ b/solution.py
@@ -86,16 +86,16 @@
 
 
 def layer_kernel(
-    x,
-    routes,
-    drop,
-    buckets,
-    qkv,
-    out_w,
-    router_w,
-    gain_attn,
-    gain_ffn,
-    bias_w,
+    x_any,
+    routes_any,
+    drop_any,
+    buckets_any,
+    qkv_any,
+    out_w_any,
+    router_w_any,
+    gain_attn_any,
+    gain_ffn_any,
+    bias_w_any,
     cot_any,
     expert_in_any,
     expert_out_any,
@@ -107,6 +107,16 @@
     result_any,
     grad_in_any,
     grad_eout_any,
+    x,
+    routes,
+    drop,
+    buckets,
+    qkv,
+    out_w,
+    router_w,
+    gain_attn,
+    gain_ffn,
+    bias_w,
     cot,
     expert_in,
     expert_out,
@@ -175,6 +185,23 @@
             ]
         )
     ]
+    early = [
+        pltpu.make_async_copy(source, target, local_sem.at[7 + i])
+        for i, (source, target) in enumerate(
+            [
+                (x_any, x),
+                (routes_any, routes),
+                (drop_any, drop),
+                (buckets_any, buckets),
+                (qkv_any, qkv),
+                (out_w_any, out_w),
+                (router_w_any, router_w),
+                (gain_attn_any, gain_attn),
+                (gain_ffn_any, gain_ffn),
+                (bias_w_any, bias_w),
+            ]
+        )
+    ]
     stores = [
         pltpu.make_async_copy(source, target, local_sem.at[4 + i])
         for i, (source, target) in enumerate(
@@ -217,8 +244,12 @@
         hello(quad + lax.rem(m + j, 4))
     for_range(1, 32, lambda j: hello(4 * lax.rem(g + j, 32) + m))
 
+    for load in early:
+        load.start()
     for load in loads:
         load.start()
+    for load in early:
+        load.wait()
     tokens[m] = x[...]
     offsets[...] = jnp.full((1, 512), -1, jnp.int32)
     offsets[:, :511] = buckets[...]
@@ -788,6 +819,16 @@
 
 
 SCRATCH = [
+    ((128, 768), BF),
+    ((1, 128), jnp.int32),
+    ((1, 128), jnp.int32),
+    ((1, 511), jnp.int32),
+    ((6, 2304), BF),
+    ((6, 768), BF),
+    ((6, 16), BF),
+    ((1, 6), BF),
+    ((1, 6), BF),
+    ((1, 3), BF),
     ((128, 768), BF),
     ((768, 384), BF),
     ((384, 768), BF),
@@ -873,13 +914,13 @@
             shape(768, 384, dtype=F32),
             shape(384, 768, dtype=F32),
         ],
-        in_specs=[vmem] * 10 + [anywhere] * 4,
+        in_specs=[pl.BlockSpec(memory_space=pltpu.HBM)] * 14,
         out_specs=[vmem] * 4 + [anywhere] * 3,
         scratch_shapes=[pltpu.VMEM(dims, dtype) for dims, dtype in SCRATCH]
         + [
             pltpu.SemaphoreType.DMA((TRANSFERS,)),
             pltpu.SemaphoreType.DMA((TRANSFERS,)),
-            pltpu.SemaphoreType.DMA((7,)),
+            pltpu.SemaphoreType.DMA((17,)),
         ],
         compiler_params=pltpu.CompilerParams(
             collective_id=0, has_side_effects=True, vmem_limit_bytes=60 * 1024 * 1024

time: 150 us -> 150 us (level)
  no operation moved by 1% of the time
where the time goes in v4:
time: 150 us; the launch traced here: 149 us
  Pallas kernels  149 us (99%)
    pallas_call x1, Pallas kernels, body(): pl.pallas_call(layer_kernel, out_shape=[shape(128, 768), shape(6, 2304, d...  144 us
    pallas_call x1, Pallas kernels, body(): pl.pallas_call(results_kernel, out_shape=[shape(128, 768), shape(128, 768...  4.04 us

profile of v4, /device:TPU:1, one launch (start us, length us, event | category | flops | bytes accessed | tf_op | source)
XLA Modules:
  0.0 149.3 jit_solution(16793374615564293206)
XLA Ops:
  0.6 144.5 %shard_map.213 = (bf16[128,768]{1,0:T(8,128)(2,1)}, f32[6,2304]{1,0:T(8,128)}, f32[6,768]{1,0:T(8,128)}, f32[8,128]{1,0:T(8,128)}, bf16[128,768]{1,0:T(8,128)(2,...) custom-call(bf16[128,768]{1,0:T(8,128)(2,1)} %x_any.1, s32[1,128]{1,0:T(1,128)} %bitcast.10, s32[1,128]{1,0:T(1,128)} %bitcast.11, ...), custom_call_target="tpu_custom_call" | custom-call | tf_op jit(solution)/shard_map/pallas_call | solution.py:906
  145.1 4.0 %shard_map.214 = (bf16[128,768]{1,0:T(8,128)(2,1)}, bf16[128,768]{1,0:T(8,128)(2,1)}, f32[6,2304]{1,0:T(8,128)}, f32[6,768]{1,0:T(8,128)}, f32[6,16]{1,0:T(8,128...) custom-call(bf16[128,768]{1,0:T(8,128)(2,1)} %get-tuple-element.27.result,, ...), custom_call_target="tpu_custom_call" | custom-call | tf_op jit(solution)/shard_map/pallas_call | solution.py:945

commit v5 on v4

--- a/solution.py
+++ b/solution.py
@@ -100,7 +100,7 @@
     expert_in_any,
     expert_out_any,
     choose_any,
-    grad_input_o,
+    grad_input_any,
     grad_qkv_o,
     grad_out_o,
     grad_small_o,
@@ -122,6 +122,7 @@
     expert_out,
     choose,
     result_s,
+    grad_input_s,
     grad_in_o,
     grad_eout_o,
     offsets,
@@ -208,6 +209,7 @@
             [(result_s, result_any), (grad_in_o, grad_in_any), (grad_eout_o, grad_eout_any)]
         )
     ]
+    last_store = pltpu.make_async_copy(grad_input_s, grad_input_any, local_sem.at[17])
     links = Links(send_sem, recv_sem)
     fs, sp = lax.axis_index("fsdp"), lax.axis_index("sp")
     f = fs * 2 + sp
@@ -706,9 +708,10 @@
     grad_wide_in[g] = grad_wide[g]
     reduce_pass(1, copies)
     values = x[...].astype(F32)
-    grad_input_o[...] = (
+    grad_input_s[...] = (
         grad_after_s[...] + rms_back(reduce_end(1, copies), values, rms_scale(values), gain_one)
     ).astype(BF)
+    last_store.start()
     for_range(0, 8, lambda q: away(q, lambda k: copy_go(k).wait_send()))
 
     @pl.when(plane == m)
@@ -732,7 +735,7 @@
     for_range(1, 32, lambda j: copy_w(j).wait())
     lay_a[...] = jnp.sum(grad_wide_in[...].astype(F32), axis=0)
 
-    for store in stores:
+    for store in stores + [last_store]:
         store.wait()
 
     for k in range(4):
@@ -833,6 +836,7 @@
     ((768, 384), BF),
     ((384, 768), BF),
     ((HALF, 8 * SLOT), BF),
+    ((128, 768), BF),
     ((128, 768), BF),
     ((768, 384), F32),
     ((384, 768), F32),
@@ -915,12 +919,12 @@
             shape(384, 768, dtype=F32),
         ],
         in_specs=[pl.BlockSpec(memory_space=pltpu.HBM)] * 14,
-        out_specs=[vmem] * 4 + [anywhere] * 3,
+        out_specs=[anywhere] + [vmem] * 3 + [anywhere] * 3,
         scratch_shapes=[pltpu.VMEM(dims, dtype) for dims, dtype in SCRATCH]
         + [
             pltpu.SemaphoreType.DMA((TRANSFERS,)),
             pltpu.SemaphoreType.DMA((TRANSFERS,)),
-            pltpu.SemaphoreType.DMA((17,)),
+            pltpu.SemaphoreType.DMA((18,)),
         ],
         compiler_params=pltpu.CompilerParams(
             collective_id=0, has_side_effects=True, vmem_limit_bytes=60 * 1024 * 1024

time: 150 us -> 150 us (level)
  no operation moved by 1% of the time
where the time goes in v5:
time: 150 us
  Pallas kernels  149 us (99%)
    pallas_call x1, Pallas kernels, body(): pl.pallas_call(layer_kernel, out_shape=[shape(128, 768), shape(6, 2304, d...  145 us
    pallas_call x1, Pallas kernels, body(): pl.pallas_call(results_kernel, out_shape=[shape(128, 768), shape(128, 768...  4.04 us

profile of v5, /device:TPU:1, one launch (start us, length us, event | category | flops | bytes accessed | tf_op | source)
XLA Modules:
  0.0 149.5 jit_solution(7414041460597058631)
XLA Ops:
  0.6 144.6 %shard_map.213 = (bf16[128,768]{1,0:T(8,128)(2,1)}, f32[6,2304]{1,0:T(8,128)}, f32[6,768]{1,0:T(8,128)}, f32[8,128]{1,0:T(8,128)}, bf16[128,768]{1,0:T(8,128)(2,...) custom-call(bf16[128,768]{1,0:T(8,128)(2,1)} %x_any.1, s32[1,128]{1,0:T(1,128)} %bitcast.10, s32[1,128]{1,0:T(1,128)} %bitcast.11, ...), custom_call_target="tpu_custom_call" | custom-call | tf_op jit(solution)/shard_map/pallas_call | solution.py:910
  145.3 4.0 %shard_map.214 = (bf16[128,768]{1,0:T(8,128)(2,1)}, bf16[128,768]{1,0:T(8,128)(2,1)}, f32[6,2304]{1,0:T(8,128)}, f32[6,768]{1,0:T(8,128)}, f32[6,16]{1,0:T(8,128...) custom-call(bf16[128,768]{1,0:T(8,128)(2,1)} %get-tuple-element.27.result,, ...), custom_call_target="tpu_custom_call" | custom-call | tf_op jit(solution)/shard_map/pallas_call | solution.py:949
